TPU v7x, 128 devices: a whole 4x4x4 slice. The times are simulated.
128 devices in a mesh: lon: 32 (over z, x, core), lat: 4 (over y).
Axes of the slice: x: 4, y: 4, z: 4, core: 2. Of those that a mesh axis runs over, the one named last changes fastest.
Arguments:
- obs_values: bfloat16 [16384, 1, 128, 128], P(('lon', 'lat')), may hold values from -6 to 6
- obs_weights: float32 [16384, 1, 128], P(('lon', 'lat')), may hold values from 0.3 to 3
- block_counts: int32 [16384, 1], P(('lon', 'lat')), may hold values from 0 to 128, as said below
- obs_cells: int32 [16384, 1, 128], P(('lon', 'lat')), may hold values from 0 to 127
- block_tiles: int32 [16384, 1], P(('lon', 'lat')), may hold values from 0 to 95
- shift_offsets: int32 [2], replicated, may hold values from 1 to 7
- embed_weight: bfloat16 [128, 128], replicated, may hold values from -0.5 to 0.5
- patch_weight: bfloat16 [2048, 1024], replicated, may hold values from -0.125 to 0.125
- norm_gain: float32 [1024], replicated, may hold values from 0.25 to 1.75
- qkv_weight: bfloat16 [1024, 3072], replicated, as said below
- proj_weight: bfloat16 [1024, 1024], replicated, may hold values from -0.1875 to 0.1875
- out_gain: float32 [1024], replicated, may hold values from 0.25 to 1.75
- unembed_weight: bfloat16 [1024, 2048], replicated, may hold values from -0.1875 to 0.1875
- read_weight: bfloat16 [128, 128], replicated, may hold values from -0.5 to 0.5
Outputs:
- obs_pred: bfloat16 [16384, 1, 128, 128], P(('lon', 'lat'))
Inputs may be any that keep to these rules, and one draw needn't show every extreme that they name: Only the first block_counts[b] slots of block b hold observations; the others are padding. `qkv_weight`: Query, key and value columns in that order, each head's 32 columns together.
All inputs are finite; a program needn't handle non-finite values.
Results may differ from a plain program's by a relative error of at most 0.014.
Values may be sent and summed in bfloat16 or wider, within the bound.
No kernel may reach another device: no remote copies, remote signals or barrier semaphores. Data moves between devices by JAX's collectives and lax.ppermute only.
A program may use at most 192 MiB of HBM per device.

v0:
```python
import jax
import jax.numpy as jnp
from jax import lax
from jax.experimental import pallas as pl
from jax.experimental.pallas import tpu as pltpu
from jax.sharding import PartitionSpec as P

CH = 128
D = 1024
HEAD = 32
CELLS = 16
WIN = 8
TILE = 128
HP = 32
WP = 24
TILES = 96
TOKENS = HP * WP
BLOCKS = 128
GROUP = 16
SPAN_R = HP + WIN
SPAN_C = WP + WIN
EXT_R = HP + 2 * WIN
WIN_TOK = WIN * WIN
LANES = 128
COLS = 256
DEAD = 1e30
GELU = 0.7978845608028654
DEAD_LIMIT = 1e6
MIB = 1024 * 1024
F32 = jnp.float32
BF16 = jnp.bfloat16


VMEM_SPEC = pl.BlockSpec(memory_space=pltpu.VMEM)
SMEM_SPEC = pl.BlockSpec(memory_space=pltpu.SMEM)
HBM_SPEC = pl.BlockSpec(memory_space=pl.ANY)


def layer_norm(values, gain_vector):
    row_mean = jnp.mean(values, axis=-1, keepdims=True)
    centered = values - row_mean
    variance = jnp.mean(centered * centered, axis=-1, keepdims=True)
    return centered * lax.rsqrt(variance + 1e-05) * gain_vector


def embed_kernel(counts_ref, weights_ref, embed_ref, values_hbm, out_hbm, values, out, in_sems, out_sems):
    parts = BLOCKS // GROUP

    def arrival(part):
        rows = pl.ds(part * GROUP, GROUP)
        return pltpu.make_async_copy(values_hbm.at[rows], values.at[rows], in_sems.at[part])

    def leave(part):
        rows = pl.ds(part * GROUP, GROUP)
        return pltpu.make_async_copy(out.at[rows], out_hbm.at[rows], out_sems.at[part])

    for part in range(parts):
        arrival(part).start()
    slot_iota = lax.broadcasted_iota(jnp.int32, (TILE, CH), 0)

    @pl.loop(0, parts)
    def _(part):
        first = pl.multiple_of(part * GROUP, GROUP)
        columns = (weights_ref[pl.ds(first, GROUP), :] * 0.5).T
        arrival(part).wait()
        for b in range(GROUP):
            raw = jnp.dot(values[first + b], embed_ref[...], preferred_element_type=F32)
            inner = jnp.tanh(raw * (GELU + GELU * 0.044715 * (raw * raw)))
            embedded = raw * columns[:, b : b + 1] * (1.0 + inner)
            out[first + b] = jnp.where(slot_iota < counts_ref[first + b], embedded, DEAD).astype(BF16)
        leave(part).start()

    for part in range(parts):
        leave(part).wait()


def embed(block_counts, obs_values, obs_weights, embed_weight):
    return pl.pallas_call(
        embed_kernel,
        in_specs=[SMEM_SPEC, VMEM_SPEC, VMEM_SPEC, HBM_SPEC],
        out_specs=HBM_SPEC,
        out_shape=jax.ShapeDtypeStruct((BLOCKS, TILE, CH), BF16),
        scratch_shapes=[
            pltpu.VMEM((BLOCKS, TILE, CH), BF16),
            pltpu.VMEM((BLOCKS, TILE, CH), BF16),
            pltpu.SemaphoreType.DMA((BLOCKS // GROUP,)),
            pltpu.SemaphoreType.DMA((BLOCKS // GROUP,)),
        ],
        compiler_params=pltpu.CompilerParams(vmem_limit_bytes=60 * MIB),
        cost_estimate=pl.CostEstimate(flops=6 * 10**8, bytes_accessed=8 * 10**6, transcendentals=2 * 10**6),
        name="embed",
    )(block_counts, obs_weights, embed_weight, obs_values)


def grid_kernel(
    tiles_ref, cells_ref, gain_ref, received_hbm, patch_hbm,
    tokens_ref, normed_ref, west_ref, east_ref, north_ref, south_ref, live_cells_ref,
    received, cell_sums, patch_rows, patch_weight, normed, sems,
):
    parts = BLOCKS // GROUP

    def arrival(part):
        rows = pl.ds(part * GROUP, GROUP)
        return pltpu.make_async_copy(received_hbm.at[rows], received.at[rows], sems.at[part])

    for part in range(parts):
        arrival(part).start()
    weight_copy = pltpu.make_async_copy(patch_hbm, patch_weight, sems.at[parts])
    weight_copy.start()

    @pl.loop(0, TILES, unroll=2)
    def _(tile):
        cell_sums[tile] = jnp.zeros((TILE, CH), F32)

    cell_iota = lax.broadcasted_iota(jnp.int32, (TILE, TILE), 0)
    slot_iota = lax.broadcasted_iota(jnp.int32, (1, TILE), 1).astype(F32)

    @pl.loop(0, parts)
    def _(part):
        arrival(part).wait()
        first = pl.multiple_of(part * GROUP, GROUP)
        all_cells = cells_ref[pl.ds(first, GROUP), :]
        all_cells = (all_cells & 15) * 8 + (all_cells >> 4)
        live_rows = []
        for b in range(GROUP):
            cells = all_cells[b : b + 1, :]
            block = received[first + b]
            live = block < jnp.asarray(DEAD_LIMIT, BF16)
            block = jnp.where(live, block, jnp.zeros_like(block))
            count = jnp.sum(jnp.where(live, 1.0, 0.0).astype(F32), axis=0, keepdims=True)
            live_rows.append(jnp.where(slot_iota < count, cells, -1))
            one_hot = jnp.where(cell_iota == cells, 1.0, 0.0).astype(BF16)
            tile = tiles_ref[first + b]
            cell_sums[tile] += jnp.dot(one_hot, block, preferred_element_type=F32)
        live_cells_ref[pl.ds(first, GROUP), :] = jnp.concatenate(live_rows, axis=0)

    weight_copy.wait()

    @pl.loop(0, 3, unroll=3)
    def _(m):
        rows = pl.ds(pl.multiple_of(m * 256, 256), 256)
        tiles = cell_sums[pl.ds(m * 32, 32)].reshape(32, CELLS, 8, CH)
        for cell in range(CELLS):
            patch_rows[rows, cell * CH : (cell + 1) * CH] = tiles[:, cell].reshape(256, CH).astype(BF16)
        part = jnp.dot(patch_rows[rows, :], patch_weight[...], preferred_element_type=F32).astype(BF16)
        tokens_ref[rows, :] = part
        values = layer_norm(part.astype(F32), gain_ref[...])
        normed[rows, :] = values
        normed_ref[rows, :] = values.astype(BF16)

    def edge(row, col):
        first = normed[pl.ds(pl.multiple_of(row * WP + col, 8), WIN), :]
        second = normed[pl.ds(pl.multiple_of((row + 1) * WP + col, 8), WIN), :]
        return jnp.concatenate([first, second], axis=0).astype(BF16)

    @pl.loop(0, HP // 2, unroll=2)
    def _(pair):
        rows = pl.ds(pl.multiple_of(pair * 16, 16), 16)
        west_ref[rows, :] = edge(pair * 2, 0)
        east_ref[rows, :] = edge(pair * 2, WP - WIN)

    @pl.loop(0, WIN // 2, unroll=2)
    def _(pair):
        for col in range(3):
            rows = pl.ds(pl.multiple_of(col * WIN_TOK + pair * 16, 16), 16)
            north_ref[rows, :] = edge(pair * 2, col * WIN)
            south_ref[rows, :] = edge(HP - WIN + pair * 2, col * WIN)


def grid_tokens(block_tiles, obs_cells, norm_gain, received, patch_weight):
    whole = lambda rows: jax.ShapeDtypeStruct((rows, D), BF16)
    outs = [whole(n) for n in (TOKENS, TOKENS, WIN * HP, WIN * HP, WIN * WP, WIN * WP)]
    outs.append(jax.ShapeDtypeStruct((BLOCKS, TILE), jnp.int32))
    return pl.pallas_call(
        grid_kernel,
        in_specs=[SMEM_SPEC, VMEM_SPEC, VMEM_SPEC, HBM_SPEC, HBM_SPEC],
        out_specs=[VMEM_SPEC] * len(outs),
        scratch_shapes=[
            pltpu.VMEM((BLOCKS, TILE, CH), BF16),
            pltpu.VMEM((TILES, TILE, CH), F32),
            pltpu.VMEM((TOKENS, CELLS * CH), BF16),
            pltpu.VMEM((CELLS * CH, D), BF16),
            pltpu.VMEM((TOKENS, D), F32),
            pltpu.SemaphoreType.DMA((BLOCKS // GROUP + 1,)),
        ],
        out_shape=outs,
        compiler_params=pltpu.CompilerParams(vmem_limit_bytes=40 * MIB),
        cost_estimate=pl.CostEstimate(flops=4 * 10**9, bytes_accessed=14 * 10**6, transcendentals=0),
        name="grid_tokens",
    )(block_tiles, obs_cells, norm_gain, received, pltpu.with_memory_space_constraint(patch_weight, pltpu.HBM))


INNER = (1, 1, 3, (1, 2))
EDGES = (0, 4, 2, (1, 2))
SIDES = (0, 1, 5, (0, 3))


def slots_of(windows):
    return windows[2] * len(windows[3])


def place(source, first, ext, across, rows, row, col, width):
    @pl.loop(0, rows // 2, unroll=2)
    def _(pair):
        both = source[pl.ds(pl.multiple_of(first + pair * 2 * width, 16), 2 * width), :].astype(F32)
        at = (row + pair * 2) * across + col
        ext[pl.ds(pl.multiple_of(at, 8), width), :] = both[:width]
        ext[pl.ds(pl.multiple_of(at + across, 8), width), :] = both[width:]


def attend(windows, meta_ref, ext, qkv_hbm, picked, qkv, qkv_weight, bias, ones, weight_sems, fill, store, later=None):
    row_shift, col_shift, special = meta_ref[0], meta_ref[1], meta_ref[2]
    first, stride, count, cols = windows
    total = slots_of(windows) * WIN_TOK

    def weights(part):
        cols = pl.ds(pl.multiple_of(part * D, D), D)
        return pltpu.make_async_copy(qkv_hbm.at[:, cols], qkv_weight.at[:, cols], weight_sems.at[part])

    for part in range(3):
        weights(part).start()
    ones[...] = (
        lax.broadcasted_iota(jnp.int32, (4 * WIN_TOK, LANES), 0) // WIN_TOK
        == lax.broadcasted_iota(jnp.int32, (4 * WIN_TOK, LANES), 1) // HEAD
    ).astype(F32).astype(BF16)
    row_step = fill()

    @pl.loop(0, count * 4, unroll=2)
    def _(pair):
        step, quarter = pair // 4, pair % 4
        row = row_step * step + quarter * 2 + row_shift
        for index, col in enumerate(cols):
            rows = []
            for half in range(2):
                if windows is SIDES:
                    at = pl.multiple_of((row + half) * 4 * WIN + index * 2 * WIN, 2 * WIN)
                    rows.append(pltpu.roll(ext[pl.ds(at, 2 * WIN), :], 2 * WIN - col_shift, 0)[:WIN])
                else:
                    at = pl.multiple_of((row + half) * WP, 8)
                    around = pltpu.roll(ext[pl.ds(at, WP), :], WP - col_shift, 0)
                    rows.append(around[index * WIN : (index + 1) * WIN])
            at = (step * len(cols) + index) * WIN_TOK + quarter * 16
            picked[pl.ds(pl.multiple_of(at, 16), 16), :] = jnp.concatenate(rows, axis=0).astype(BF16)

    block = total // 2 if total > 512 else total

    @pl.loop(0, 3)
    def _(n):
        weights(n).wait()
        lanes = pl.ds(pl.multiple_of(n * D, D), D)

        @pl.loop(0, total // block, unroll=total // block)
        def _(m):
            rows = pl.ds(pl.multiple_of(m * block, block), block)
            qkv[rows, lanes] = jnp.dot(
                picked[rows, :], qkv_weight[:, lanes], preferred_element_type=F32
            ).astype(BF16)

    if later is not None:
        later()
    edge_rows = first == 0
    if edge_rows:

        @pl.loop(0, WIN)
        def _(i):
            query_flag = jnp.where(i >= WIN - row_shift, 1, 0)
            key_row = (lax.broadcasted_iota(jnp.int32, (WIN, LANES), 1) % WIN_TOK) // WIN
            key_flag = jnp.where(key_row >= WIN - row_shift, 1, 0)
            bias[1, pl.ds(pl.multiple_of(i * WIN, 8), WIN), :] = jnp.where(key_flag == query_flag, 0.0, 1.0)

        bias[0] = jnp.zeros((WIN_TOK, LANES), F32)

    @pl.loop(0, count, unroll=count)
    def _(step):
        mask = bias.at[jnp.where(first + stride * step == special, 1, 0)] if edge_rows else None

        @pl.loop(0, D // LANES, unroll=8)
        def _(group):
            for index in range(len(cols)):
                result = attention_group(qkv, mask, ones, step * len(cols) + index, group)
                lanes = pl.ds(pl.multiple_of(group * LANES, LANES), LANES)
                for i in range(WIN):
                    store(step, index, i, lanes, result[i * WIN : (i + 1) * WIN])


def attention_group(qkv, mask, ones, slot, group):
    rows = pl.ds(pl.multiple_of(slot * WIN_TOK, WIN_TOK), WIN_TOK)
    lanes = lambda part: pl.ds(pl.multiple_of(part * D + group * LANES, LANES), LANES)
    query, key, value = (qkv[rows, lanes(part)] for part in range(3))
    head_of_lane = lax.broadcasted_iota(jnp.int32, (WIN_TOK, LANES), 1) // HEAD
    zero = jnp.zeros((WIN_TOK, LANES), BF16)
    spread = lambda x: jnp.concatenate([jnp.where(head_of_lane == h, x, zero) for h in range(4)], axis=0)
    scores = lax.dot_general(
        query, spread(key), (((1,), (1,)), ((), ())), preferred_element_type=F32
    ) * HEAD ** (-0.5)
    low = lax.broadcasted_iota(jnp.int32, (WIN_TOK, LANES), 1) < WIN_TOK
    parts = []
    for half in range(2):
        part = scores[:, half * LANES : (half + 1) * LANES]
        if mask is not None:
            part = jnp.where(mask[...] < 0.5, part, -1000000000.0)
        low_max = jnp.max(jnp.where(low, part, -jnp.inf), axis=-1, keepdims=True)
        high_max = jnp.max(jnp.where(low, -jnp.inf, part), axis=-1, keepdims=True)
        parts.append(jnp.exp(part - jnp.where(low, low_max, high_max)).astype(BF16))
    weights = jnp.concatenate(parts, axis=1)
    both = jnp.dot(weights, jnp.concatenate([spread(value), ones[...]], axis=1), preferred_element_type=F32)
    return (both[:, :LANES] / both[:, LANES:]).astype(BF16).astype(F32)


def windows_kernel(windows, *refs):
    meta_ref, *sources, qkv_hbm, out, ext, picked, qkv, qkv_weight, bias, ones, weight_sems = refs

    def fill():
        if windows is INNER:
            place(sources[0], 0, ext, WP, HP, 0, 0, WP)
            return WIN
        for index, source in enumerate(sources):
            for col in range(3):
                place(source, col * WIN_TOK, ext, WP, WIN, index * WIN, col * WIN, WIN)
        return 2 * WIN

    def store(step, index, i, lanes, value):
        out[step * WIN + i, index * WIN : (index + 1) * WIN, lanes] = value

    attend(windows, meta_ref, ext, qkv_hbm, picked, qkv, qkv_weight, bias, ones, weight_sems, fill, store)


def attend_scratch(windows):
    rows = slots_of(windows) * WIN_TOK
    return [
        pltpu.VMEM((EXT_R * 4 * WIN if windows is SIDES else HP * WP, D), F32),
        pltpu.VMEM((rows, D), BF16),
        pltpu.VMEM((rows, 3 * D), BF16),
        pltpu.VMEM((D, 3 * D), BF16),
        pltpu.VMEM((2, WIN_TOK, LANES), F32),
        pltpu.VMEM((4 * WIN_TOK, LANES), BF16),
        pltpu.SemaphoreType.DMA((3,)),
    ]


def attend_windows(windows, name, meta, sources, qkv_weight):
    rows = slots_of(windows) * WIN_TOK
    return pl.pallas_call(
        lambda *refs: windows_kernel(windows, *refs),
        in_specs=[SMEM_SPEC] + [VMEM_SPEC] * len(sources) + [HBM_SPEC],
        out_specs=VMEM_SPEC,
        out_shape=jax.ShapeDtypeStruct((windows[2] * WIN, 2 * WIN, D), F32),
        scratch_shapes=attend_scratch(windows),
        compiler_params=pltpu.CompilerParams(vmem_limit_bytes=28 * MIB),
        cost_estimate=pl.CostEstimate(
            flops=rows * D * 3 * D * 3, bytes_accessed=12 * 10**6, transcendentals=rows * 2048
        ),
        name=name,
    )(meta, *sources, qkv_weight)


def tail_kernel(
    meta_ref, tiles_ref, cells_ref, tokens_hbm, west_ref, east_ref, from_west_ref, from_east_ref,
    inner_hbm, edges_hbm, out_gain_ref, read_ref, qkv_hbm, proj_hbm, unembed_hbm,
    out_hbm,
    ext, picked, qkv, qkv_weight, bias, ones, weight_sems,
    mixed, mixed_rows, tokens, decoded, out_stage, read_pair,
    proj_weight, unembed_weight, in_sems, out_sems,
):
    row_shift, col_shift = meta_ref[0], meta_ref[1]
    inner_cols = pl.ds(WIN, 2 * WIN)
    moves = (
        (inner_hbm, mixed.at[pl.ds(WIN, 3 * WIN), inner_cols, :]),
        (edges_hbm.at[pl.ds(0, WIN)], mixed.at[pl.ds(0, WIN), inner_cols, :]),
        (edges_hbm.at[pl.ds(WIN, WIN)], mixed.at[pl.ds(SPAN_R - WIN, WIN), inner_cols, :]),
        (proj_hbm, proj_weight),
        (tokens_hbm, tokens),
        (unembed_hbm, unembed_weight),
    )
    copies = [pltpu.make_async_copy(src, dst, in_sems.at[i]) for i, (src, dst) in enumerate(moves)]

    def fill():
        place(from_west_ref, 0, ext, 4 * WIN, EXT_R, 0, 0, WIN)
        place(west_ref, 0, ext, 4 * WIN, EXT_R, 0, WIN, WIN)
        place(east_ref, 0, ext, 4 * WIN, EXT_R, 0, 2 * WIN, WIN)
        place(from_east_ref, 0, ext, 4 * WIN, EXT_R, 0, 3 * WIN, WIN)
        read_pair[...] = jnp.zeros((2 * CH, 2 * CH), BF16)
        read_pair[:CH, :CH] = read_ref[...]
        read_pair[CH:, CH:] = read_ref[...]
        return WIN

    def store(step, index, i, lanes, value):
        mixed[step * WIN + i, index * 3 * WIN : index * 3 * WIN + WIN, lanes] = value

    def later():
        for copy in copies:
            copy.start()

    attend(SIDES, meta_ref, ext, qkv_hbm, picked, qkv, qkv_weight, bias, ones, weight_sems, fill, store, later)
    for copy in copies[:5]:
        copy.wait()

    @pl.loop(0, HP // 2, unroll=2)
    def _(pair):
        rows = [
            pltpu.roll(mixed[WIN - row_shift + pair * 2 + half], SPAN_C - WIN + col_shift, 0)[:WP]
            for half in range(2)
        ]
        mixed_rows[pl.ds(pl.multiple_of(pair * 2 * WP, 2 * WP), 2 * WP), :] = jnp.concatenate(
            rows, axis=0
        ).astype(BF16)

    @pl.loop(0, TOKENS // 256, unroll=3)
    def _(m):
        rows = pl.ds(pl.multiple_of(m * 256, 256), 256)
        change = jnp.dot(mixed_rows[rows, :], proj_weight[...], preferred_element_type=F32)
        updated = (change + tokens[rows, :].astype(F32)).astype(BF16).astype(F32)
        mixed_rows[rows, :] = layer_norm(updated, out_gain_ref[...]).astype(BF16)

    copies[5].wait()

    @pl.loop(0, 2)
    def _(n):
        cols = pl.ds(pl.multiple_of(n * D, D), D)

        @pl.loop(0, 3, unroll=3)
        def _(m):
            rows = pl.ds(pl.multiple_of(m * 256, 256), 256)
            quad = jnp.dot(
                mixed_rows[rows, :], unembed_weight[:, cols], preferred_element_type=F32
            ).astype(BF16)
            for k in range(4):
                cells = jnp.dot(
                    quad[:, k * COLS : (k + 1) * COLS], read_pair[...], preferred_element_type=F32
                )
                pair = jnp.concatenate(
                    [cells[:, :CH].reshape(32, 8, CH), cells[:, CH:].reshape(32, 8, CH)], axis=1
                ).astype(BF16)
                place_at = pl.multiple_of(n * 64 + k * 16, 16)
                decoded[pl.ds(m * 32, 32), pl.ds(place_at, 16), :] = pair

    cell_iota = lax.broadcasted_iota(jnp.int32, (TILE, TILE), 0)

    def leave(part):
        return pltpu.make_async_copy(
            out_stage.at[part % 2], out_hbm.at[pl.ds(part * GROUP, GROUP)], out_sems.at[part % 2]
        )

    @pl.loop(0, BLOCKS // GROUP)
    def _(part):
        @pl.when(part >= 2)
        def _():
            leave(part - 2).wait()

        for b in range(GROUP):
            block = part * GROUP + b
            cells = cells_ref[pl.ds(block, 1), :]
            one_hot = jnp.where(cell_iota == cells, 1.0, 0.0).astype(BF16)
            out_stage[part % 2, b] = lax.dot_general(
                one_hot, decoded[tiles_ref[block]], (((0,), (0,)), ((), ())), preferred_element_type=F32
            ).astype(BF16)
        leave(part).start()

    for part in range(BLOCKS // GROUP - 2, BLOCKS // GROUP):
        leave(part).wait()


def tail(meta, block_tiles, live_cells, tokens, sides, mixed_parts, out_gain, read_weight, qkv_weight, proj_weight, unembed_weight):
    return pl.pallas_call(
        tail_kernel,
        in_specs=[SMEM_SPEC, SMEM_SPEC] + [VMEM_SPEC, HBM_SPEC] + [VMEM_SPEC] * 4 + [HBM_SPEC] * 2 + [VMEM_SPEC] * 2 + [HBM_SPEC] * 3,
        out_specs=HBM_SPEC,
        out_shape=jax.ShapeDtypeStruct((BLOCKS, TILE, CH), BF16),
        scratch_shapes=attend_scratch(SIDES)
        + [
            pltpu.VMEM((SPAN_R, SPAN_C, D), F32),
            pltpu.VMEM((TOKENS, D), BF16),
            pltpu.VMEM((TOKENS, D), BF16),
            pltpu.VMEM((TILES, TILE, CH), BF16),
            pltpu.VMEM((2, GROUP, TILE, CH), BF16),
            pltpu.VMEM((2 * CH, 2 * CH), BF16),
            pltpu.VMEM((D, D), BF16),
            pltpu.VMEM((D, 2 * D), BF16),
            pltpu.SemaphoreType.DMA((6,)),
            pltpu.SemaphoreType.DMA((2,)),
        ],
        compiler_params=pltpu.CompilerParams(vmem_limit_bytes=46 * MIB),
        cost_estimate=pl.CostEstimate(flops=12 * 10**9, bytes_accessed=28 * 10**6, transcendentals=10**6),
        name="sides_decode",
    )(
        meta, block_tiles, live_cells, pltpu.with_memory_space_constraint(tokens, pltpu.HBM), *sides, *mixed_parts,
        out_gain, read_weight, qkv_weight, proj_weight, unembed_weight,
    )


def send(value, lon_step, lat_step):
    lon, lat = lax.axis_size("lon"), lax.axis_size("lat")
    pairs = [
        (i * lat + j, (i + lon_step) % lon * lat + (j + lat_step) % lat) for i in range(lon) for j in range(lat)
    ]
    return lax.ppermute(value, ("lon", "lat"), pairs)


def attention_and_decode(meta, block_tiles, live_cells, tokens, normed, west, east, north, south, out_gain, read_weight, qkv_weight, proj_weight, unembed_weight):
    from_north, from_south = send(south, 0, 1), send(north, 0, -1)
    inner = attend_windows(INNER, "inner_windows", meta, (normed,), qkv_weight)
    from_north, from_south, inner = lax.optimization_barrier((from_north, from_south, inner))
    west = jnp.concatenate([from_north[:WIN_TOK], west, from_south[:WIN_TOK]], axis=0)
    east = jnp.concatenate([from_north[2 * WIN_TOK :], east, from_south[2 * WIN_TOK :]], axis=0)
    from_west, from_east = send(east, 1, 0), send(west, -1, 0)
    edges = attend_windows(EDGES, "edge_windows", meta, (from_north, north, south, from_south), qkv_weight)
    from_west, from_east, edges = lax.optimization_barrier((from_west, from_east, edges))
    return tail(
        meta, block_tiles, live_cells, tokens, (west, east, from_west, from_east), (inner, edges),
        out_gain, read_weight, qkv_weight, proj_weight, unembed_weight,
    )


def per_device(
    obs_values,
    obs_weights,
    block_counts,
    obs_cells,
    block_tiles,
    shift_offsets,
    embed_weight,
    patch_weight,
    norm_gain,
    qkv_weight,
    proj_weight,
    out_gain,
    unembed_weight,
    read_weight,
):
    outgoing = embed(
        block_counts.reshape(BLOCKS), obs_values.reshape(BLOCKS, TILE, CH), obs_weights.reshape(BLOCKS, TILE), embed_weight
    ).reshape(BLOCKS, 1, TILE, CH)
    received = lax.all_to_all(outgoing, ("lon", "lat"), split_axis=0, concat_axis=0, tiled=True)
    block_tiles = block_tiles.reshape(BLOCKS)
    tokens, normed, west, east, north, south, live_cells = grid_tokens(
        block_tiles, obs_cells.reshape(BLOCKS, TILE), norm_gain.reshape(1, D),
        received.reshape(BLOCKS, TILE, CH), patch_weight,
    )
    lat_index = lax.axis_index("lat")
    last = lax.axis_size("lat") - 1
    special = jnp.where(lat_index == 0, 0, jnp.where(lat_index == last, 4, -1)).astype(jnp.int32)
    meta = jnp.concatenate([shift_offsets, special.reshape(1)])
    sampled = attention_and_decode(
        meta, block_tiles, live_cells, tokens, normed, west, east, north, south,
        out_gain.reshape(1, D), read_weight, qkv_weight, proj_weight, unembed_weight,
    )
    returned = lax.all_to_all(
        sampled.reshape(BLOCKS, 1, TILE, CH), ("lon", "lat"), split_axis=0, concat_axis=0, tiled=True
    )
    return returned


def solution(mesh):
    rows = ("lon", "lat")
    in_specs = (
        P(rows, None, None, None),
        P(rows, None, None),
        P(rows, None),
        P(rows, None, None),
        P(rows, None),
    ) + (P(),) * 9
    out_specs = P(rows, None, None, None)
    return jax.shard_map(
        per_device, mesh=mesh, in_specs=in_specs, out_specs=out_specs, check_vma=False
    )
```

profile of v0, /device:TPU:1, one launch (start us, length us, event | category | flops | bytes accessed | tf_op | source)
XLA Modules:
  0.0 194.7 jit_solution(8323285362414633783)
XLA Ops:
  0.0 7.9 %embed.1 = bf16[128,128,128]{2,1,0:T(8,128)(2,1)} custom-call(s32[128]{0:T(128)} %bitcast.26, f32[128,128]{1,0:T(8,128)} %bitcast.25, bf16[128,128]{1,0:T(8,128)(2,1)} %embed_ref.1, bf16[128,128,128]{2,1,0:T(8,128)(2,1)} %bitcast.23), custom_call_target="tpu_custom_call" | custom-call | flops 600000000 | bytes 8000000 | tf_op jit(solution)/shard_map/embed/pallas_call | solution.py:78
  7.9 0.0 copy-start.3
  7.9 0.0 copy-start.5
  8.0 0.0 slice-start
  8.0 12.0 %all-to-all-start = ((bf16[128,1,128,128]{3,2,1,0:T(8,128)(2,1)}), bf16[128,1,128,128]{3,2,1,0:T(8,128)(2,1)}, u32[]{:S(2)}, u32[]{:S(2)}) async-start(bf16[128,1,128,128]{3,2,1,0:T(8,128)(2,1)} %bitcast.22), calls=%async_computation | async-start | bytes 8388608 | tf_op jit(solution)/shard_map/all_to_all | solution.py:533
  20.0 52.8 %all-to-all-done = bf16[128,1,128,128]{3,2,1,0:T(8,128)(2,1)} async-done(((bf16[128,1,128,128]{3,2,1,0:T(8,128)(2,1)}), bf16[128,1,128,128]{3,2,1,0:T(8,128)(2,1)}, u32[]{:S(2)}, u32[]{:S(2)}) %all-to-all-start) | async-done | bytes 4194336 | tf_op jit(solution)/shard_map/all_to_all | solution.py:533
  72.8 0.0 slice-start.1
  72.8 10.1 %grid_tokens.1 = (bf16[768,1024]{1,0:T(8,128)(2,1)S(1)}, bf16[768,1024]{1,0:T(8,128)(2,1)S(1)}, bf16[256,1024]{1,0:T(8,128)(2,1)S(1)}, bf16[256,1024]{1,0:T(8,12...) custom-call(s32[128]{0:T(128)S(1)} %bitcast.20, ...), custom_call_target="tpu_custom_call" | custom-call | flops 4000000000 | bytes 14000000 | tf_op jit(solution)/shard_map/grid_tokens/pallas_call | solution.py:174
  83.0 1.2 copy-done.8
  84.1 0.3 collective-permute-start
  84.5 2.3 %collective-permute-start.1 = (bf16[192,1024]{1,0:T(8,128)(2,1)S(1)}, bf16[192,1024]{1,0:T(8,128)(2,1)S(1)}, u32[]{:S(2)}, u32[]{:S(2)}) collective-permute-start(bf16[192,1024]{1,0:T(8,128)(2,1)S(1)} %get-tuple-element.21.refs_2_), channel_id=1, source_target_pairs={{0,3},{1,0},{2,1},{3,2},{4,7},{5,4},{6,5},{7,6},{8,11},{9,8},{10,9... | collective-permute-start | bytes 1179656 | tf_op jit(solution)/shard_map/ppermute | solution.py:496
  86.8 0.1 pad_add_fusion.refs_0_.meta_ref
  86.9 7.4 %inner_windows.1.inner_hbm = f32[24,16,1024]{2,1,0:T(8,128)S(1)} custom-call(s32[3]{0:T(128)S(1)} %pad_add_fusion.refs_0_.meta_ref, bf16[768,1024]{1,0:T(8,128)(2,1)S(1)} %get-tuple-element.22.refs_1_, bf16[1024,3072]{1,0:T(8,128)(2,1)S(1)} %bitcast.16), custom_call_target="tpu_custom_call" | custom-call | flops 3623878656 | bytes 12000000 | tf_op jit(solution)/shard_map/inner_windows/pallas_call | solution.py:343
  94.3 1.9 collective-permute-done.refs_1_
  96.3 0.1 pad_maximum_fusion.west_ref
  96.3 0.7 collective-permute-start.3
  97.0 0.1 pad_maximum_fusion.1.east_ref
  97.1 0.0 copy-start.4
  97.1 1.3 collective-permute-start.2
  98.5 5.9 %edge_windows.1.edges_hbm = f32[16,16,1024]{2,1,0:T(8,128)S(1)} custom-call(s32[3]{0:T(128)S(1)} %pad_add_fusion.refs_0_.meta_ref, bf16[192,1024]{1,0:T(8,128)(2,1)S(1)} %collective-permute-done.refs_1_, bf16[192,1024]{1,0:T(8,128)(2,1)S(1)} %get-tuple-element.21.refs_2_, bf16[192,1024]{1,0:T(8,128)(2,1)S(1)} %get-tuple-element.20.refs_3_, ...), custom_call_target="tpu_custom_call" | custom-call | flops 2415919104 | bytes 12000000 | tf_op jit(solution)/shard_map/edge_windows/pallas_call | solution.py:343
  104.4 3.7 %collective-permute-done.3.from_east_ref = bf16[384,1024]{1,0:T(8,128)(2,1)S(1)} collective-permute-done((bf16[384,1024]{1,0:T(8,128)(2,1)S(1)}, bf16[384,1024]{1,0:T(8,128)(2,1)S(1)}, u32[]{:S(2)}, u32[]{:S(2)}) %collective-permute-start.3) | collective-permute-done | bytes 786464 | tf_op jit(solution)/shard_map/ppermute | solution.py:496
  108.1 23.2 %sides_decode.1 = bf16[128,128,128]{2,1,0:T(8,128)(2,1)} custom-call(s32[3]{0:T(128)S(1)} %pad_add_fusion.refs_0_.meta_ref, s32[128]{0:T(128)S(1)} %bitcast.21, s32[128,128]{1,0:T(8,128)S(1)} %get-tuple-element.18.cells_ref, bf16[768,1024]{1,0:T(8,128)(2,1)} %copy-done.8, bf16[384,1024]{1,0:T(8,128)(2,1)S(1)} %pad_maximum_fusion.west_ref, ...), custom_call_target="tpu_custom_call" | custom-call | flops 12000000000 | bytes 28000000 | tf_op jit(solution)/shard_map/sides_decode/pallas_call | solution.py:464
  131.3 61.4 %all_to_all.10 = bf16[128,1,128,128]{3,2,1,0:T(8,128)(2,1)S(1)} all-to-all(bf16[128,1,128,128]{3,2,1,0:T(8,128)(2,1)} %bitcast.24), channel_id=1, replica_groups=mesh['lon'=32,'lat'=4] {'lon','lat'}, dimensions={0} | all-to-all | bytes 8388608 | tf_op jit(solution)/shard_map/all_to_all | solution.py:547
  192.7 2.0 %copy.19 = bf16[128,1,128,128]{3,2,1,0:T(8,128)(2,1)} copy(bf16[128,1,128,128]{3,2,1,0:T(8,128)(2,1)S(1)} %all_to_all.10) | data formatting | bytes 8388608
  (22 shorter events, 0.1 us)
Async XLA Ops:
  7.9 64.9 %copy-start.1 = (s32[128,1,128]{2,1,0:T(1,128)S(1)}, s32[128,1,128]{2,1,0:T(1,128)}, u32[]{:S(2)}) copy-start(s32[128,1,128]{2,1,0:T(1,128)} %param.17) | copy-start | bytes 196612
  7.9 64.9 %copy-start.3 = (f32[1024]{0:T(1024)S(1)}, f32[1024]{0:T(1024)}, u32[]{:S(2)}) copy-start(f32[1024]{0:T(1024)} %param.22) | copy-start | bytes 12292
  7.9 64.9 %copy-start.5 = (s32[128,1]{0,1:T(1,128)S(1)}, s32[128,1]{0,1:T(1,128)}, u32[]{:S(2)}) copy-start(s32[128,1]{0,1:T(1,128)} %param.18) | copy-start | bytes 1540
  8.0 78.9 %slice-start = ((s8[6291456]{0:T(1024)(128)(4,1)}), s8[2097152]{0:T(1024)(128)(4,1)S(1)}, s32[]{:S(2)}) async-start(s8[6291456]{0:T(1024)(128)(4,1)} %bitcast.15), calls=%async_computation.2 | async-start | bytes 4194304
  8.0 64.8 %all-to-all-start = ((bf16[128,1,128,128]{3,2,1,0:T(8,128)(2,1)}), bf16[128,1,128,128]{3,2,1,0:T(8,128)(2,1)}, u32[]{:S(2)}, u32[]{:S(2)}) async-start(bf16[128,1,128,128]{3,2,1,0:T(8,128)(2,1)} %bitcast.22), calls=%async_computation | async-start | bytes 8388608 | tf_op jit(solution)/shard_map/all_to_all | solution.py:533
  72.8 14.0 %copy-start.9 = (s32[2]{0:T(128)S(1)}, s32[2]{0:T(128)}, u32[]{:S(2)}) copy-start(s32[2]{0:T(128)} %param.19) | copy-start | bytes 28
  72.8 14.1 %slice-start.1 = ((s8[6291456]{0:T(1024)(128)(4,1)}), s8[4194304]{0:T(1024)(128)(4,1)S(1)}, s32[]{:S(2)}) async-start(s8[6291456]{0:T(1024)(128)(4,1)} %bitcast.15), calls=%async_computation.3 | async-start | bytes 8388608
  82.9 1.2 copy-start.8
  84.1 12.1 %collective-permute-start = (bf16[192,1024]{1,0:T(8,128)(2,1)S(1)}, bf16[192,1024]{1,0:T(8,128)(2,1)S(1)}, u32[]{:S(2)}, u32[]{:S(2)}) collective-permute-start(bf16[192,1024]{1,0:T(8,128)(2,1)S(1)} %get-tuple-element.20.refs_3_), channel_id=1, source_target_pairs={{0,1},{1,2},{2,3},{3,0},{4,5},{5,6},{6,7},{7,4},{8,9},{9,10},{10,1... | collective-permute-start | bytes 1179656 | tf_op jit(solution)/shard_map/ppermute | solution.py:496
  84.5 11.7 %collective-permute-start.1 = (bf16[192,1024]{1,0:T(8,128)(2,1)S(1)}, bf16[192,1024]{1,0:T(8,128)(2,1)S(1)}, u32[]{:S(2)}, u32[]{:S(2)}) collective-permute-start(bf16[192,1024]{1,0:T(8,128)(2,1)S(1)} %get-tuple-element.21.refs_2_), channel_id=1, source_target_pairs={{0,3},{1,0},{2,1},{3,2},{4,7},{5,4},{6,5},{7,6},{8,11},{9,8},{10,9... | collective-permute-start | bytes 1179656 | tf_op jit(solution)/shard_map/ppermute | solution.py:496
  94.3 2.8 %copy-start.6 = (f32[24,16,1024]{2,1,0:T(8,128)}, f32[24,16,1024]{2,1,0:T(8,128)S(1)}, u32[]{:S(2)}) copy-start(f32[24,16,1024]{2,1,0:T(8,128)S(1)} %inner_windows.1.inner_hbm) | copy-start | bytes 4718596
  96.3 11.8 %collective-permute-start.3 = (bf16[384,1024]{1,0:T(8,128)(2,1)S(1)}, bf16[384,1024]{1,0:T(8,128)(2,1)S(1)}, u32[]{:S(2)}, u32[]{:S(2)}) collective-permute-start(bf16[384,1024]{1,0:T(8,128)(2,1)S(1)} %pad_maximum_fusion.west_ref), channel_id=1, source_target_pairs={{0,124},{1,125},{2,126},{3,127},{4,0},{5,1},{6,2},{7,3},{8,4},{9,5... | collective-permute-start | bytes 2359304 | tf_op jit(solution)/shard_map/ppermute | solution.py:496
  97.1 11.0 %copy-start = (bf16[1024,1024]{1,0:T(8,128)(2,1)S(1)}, bf16[1024,1024]{1,0:T(8,128)(2,1)}, u32[]{:S(2)}) copy-start(bf16[1024,1024]{1,0:T(8,128)(2,1)} %proj_hbm.1) | copy-start | bytes 6291460
  97.1 11.0 %copy-start.2 = (bf16[128,128]{1,0:T(8,128)(2,1)S(1)}, bf16[128,128]{1,0:T(8,128)(2,1)}, u32[]{:S(2)}) copy-start(bf16[128,128]{1,0:T(8,128)(2,1)} %read_ref.1) | copy-start | bytes 98308
  97.1 11.0 %copy-start.4 = (f32[1024]{0:T(1024)S(1)}, f32[1024]{0:T(1024)}, u32[]{:S(2)}) copy-start(f32[1024]{0:T(1024)} %param.25) | copy-start | bytes 12292
  97.1 11.0 %copy-start.7 = (f32[24,16,1024]{2,1,0:T(8,128)S(1)}, f32[24,16,1024]{2,1,0:T(8,128)}, u32[]{:S(2)}) copy-start(f32[24,16,1024]{2,1,0:T(8,128)} %copy-done.6) | copy-start | bytes 4718596
  97.1 11.0 %collective-permute-start.2 = (bf16[384,1024]{1,0:T(8,128)(2,1)S(1)}, bf16[384,1024]{1,0:T(8,128)(2,1)S(1)}, u32[]{:S(2)}, u32[]{:S(2)}) collective-permute-start(bf16[384,1024]{1,0:T(8,128)(2,1)S(1)} %pad_maximum_fusion.1.east_ref), channel_id=1, source_target_pairs={{0,4},{1,5},{2,6},{3,7},{4,8},{5,9},{6,10},{7,11},{8,12},{9,13},{1... | collective-permute-start | bytes 2359304 | tf_op jit(solution)/shard_map/ppermute | solution.py:496
where the time goes:
time: 195 us
  blocking collectives  61.4 us (31%)
  waiting for transfers between devices  58.5 us (30%)
  Pallas kernels  54.4 us (28%)
  starting transfers between devices  16.7 us (9%)
  local copies, waits for them, and re-layouts  3.28 us (2%)
    all_to_all x1, blocking collectives, per_device(): lax.all_to_all(sampled.reshape(BLOCKS, 1, TILE, CH), ('lon', 'lat'), spli...  61.4 us
    all_to_all x1, waiting for transfers between devices, per_device(): lax.all_to_all(outgoing, ('lon', 'lat'), split_axis=0, concat_axis=0, til...  52.8 us
    pallas_call x1, Pallas kernels, tail(): pl.pallas_call(tail_kernel, in_specs=[SMEM_SPEC, SMEM_SPEC] + [VMEM_SPEC,...  23.2 us
    pallas_call x2, Pallas kernels, attend_windows(): pl.pallas_call(lambda *refs: windows_kernel(windows, *refs), in_specs=[SM...  13.3 us
    all_to_all x1, starting transfers between devices, per_device(): lax.all_to_all(outgoing, ('lon', 'lat'), split_axis=0, concat_axis=0, til...  12 us
    pallas_call x1, Pallas kernels, grid_tokens(): pl.pallas_call(grid_kernel, in_specs=[SMEM_SPEC, VMEM_SPEC, VMEM_SPEC, HB...  10.1 us
    pallas_call x1, Pallas kernels, embed(): pl.pallas_call(embed_kernel, in_specs=[SMEM_SPEC, VMEM_SPEC, VMEM_SPEC, H...  7.91 us
    ppermute x4, waiting for transfers between devices, send(): return lax.ppermute(value, ('lon', 'lat'), pairs)  5.66 us
  transfers between devices with their start and end apart: 5, of which 3 were waited for; matrix products, arithmetic and copies ran while one was open for 0% of the time, Pallas kernels for 7%

commit v1 on v0

--- a/solution.py
+++ b/solution.py
@@ -25,6 +25,8 @@
 COLS = 256
 DEAD = 1e30
 GELU = 0.7978845608028654
+EXCLUDED = -1e9 * HEAD**0.5
+EXP_SCALE = 1.4426950408889634 * HEAD**-0.5
 DEAD_LIMIT = 1e6
 MIB = 1024 * 1024
 F32 = jnp.float32
@@ -34,6 +36,10 @@
 VMEM_SPEC = pl.BlockSpec(memory_space=pltpu.VMEM)
 SMEM_SPEC = pl.BlockSpec(memory_space=pltpu.SMEM)
 HBM_SPEC = pl.BlockSpec(memory_space=pl.ANY)
+
+
+def in_hbm(value):
+    return pltpu.with_memory_space_constraint(value, pltpu.HBM)
 
 
 def layer_norm(values, gain_vector):
@@ -43,16 +49,12 @@
     return centered * lax.rsqrt(variance + 1e-05) * gain_vector
 
 
-def embed_kernel(counts_ref, weights_ref, embed_ref, values_hbm, out_hbm, values, out, in_sems, out_sems):
+def embed_kernel(counts_ref, weights_ref, embed_ref, values_hbm, out, values, in_sems):
     parts = BLOCKS // GROUP
 
     def arrival(part):
         rows = pl.ds(part * GROUP, GROUP)
         return pltpu.make_async_copy(values_hbm.at[rows], values.at[rows], in_sems.at[part])
-
-    def leave(part):
-        rows = pl.ds(part * GROUP, GROUP)
-        return pltpu.make_async_copy(out.at[rows], out_hbm.at[rows], out_sems.at[part])
 
     for part in range(parts):
         arrival(part).start()
@@ -68,34 +70,28 @@
             inner = jnp.tanh(raw * (GELU + GELU * 0.044715 * (raw * raw)))
             embedded = raw * columns[:, b : b + 1] * (1.0 + inner)
             out[first + b] = jnp.where(slot_iota < counts_ref[first + b], embedded, DEAD).astype(BF16)
-        leave(part).start()
-
-    for part in range(parts):
-        leave(part).wait()
 
 
 def embed(block_counts, obs_values, obs_weights, embed_weight):
     return pl.pallas_call(
         embed_kernel,
         in_specs=[SMEM_SPEC, VMEM_SPEC, VMEM_SPEC, HBM_SPEC],
-        out_specs=HBM_SPEC,
-        out_shape=jax.ShapeDtypeStruct((BLOCKS, TILE, CH), BF16),
+        out_specs=VMEM_SPEC,
+        out_shape=pltpu.VMEM((BLOCKS, TILE, CH), BF16),
         scratch_shapes=[
             pltpu.VMEM((BLOCKS, TILE, CH), BF16),
-            pltpu.VMEM((BLOCKS, TILE, CH), BF16),
-            pltpu.SemaphoreType.DMA((BLOCKS // GROUP,)),
             pltpu.SemaphoreType.DMA((BLOCKS // GROUP,)),
         ],
-        compiler_params=pltpu.CompilerParams(vmem_limit_bytes=60 * MIB),
+        compiler_params=pltpu.CompilerParams(vmem_limit_bytes=24 * MIB),
         cost_estimate=pl.CostEstimate(flops=6 * 10**8, bytes_accessed=8 * 10**6, transcendentals=2 * 10**6),
         name="embed",
-    )(block_counts, obs_weights, embed_weight, obs_values)
+    )(in_hbm(block_counts), in_hbm(obs_weights), in_hbm(embed_weight), in_hbm(obs_values))
 
 
 def grid_kernel(
     tiles_ref, cells_ref, gain_ref, received_hbm, patch_hbm,
-    tokens_ref, normed_ref, west_ref, east_ref, north_ref, south_ref, live_cells_ref,
-    received, cell_sums, patch_rows, patch_weight, normed, sems,
+    tokens_hbm, normed_hbm, west_ref, east_ref, north_ref, south_ref, live_cells_ref,
+    received, cell_sums, patch_rows, patch_weight, tokens, normed, sems, out_sems,
 ):
     parts = BLOCKS // GROUP
 
@@ -135,59 +131,63 @@
         live_cells_ref[pl.ds(first, GROUP), :] = jnp.concatenate(live_rows, axis=0)
 
     weight_copy.wait()
-
-    @pl.loop(0, 3, unroll=3)
-    def _(m):
-        rows = pl.ds(pl.multiple_of(m * 256, 256), 256)
-        tiles = cell_sums[pl.ds(m * 32, 32)].reshape(32, CELLS, 8, CH)
+    half_rows = HP // 2
+    block = half_rows * WP
+
+    def leave(m):
+        rows = pl.ds(m * block, block)
+        return (
+            pltpu.make_async_copy(tokens.at[rows], tokens_hbm.at[rows], out_sems.at[2 * m]),
+            pltpu.make_async_copy(normed.at[rows], normed_hbm.at[rows], out_sems.at[2 * m + 1]),
+        )
+
+    for m in range(2):
+        rows = slice(m * block, (m + 1) * block)
+        tiles = cell_sums[m * (TILES // 2) : (m + 1) * (TILES // 2)].reshape(TILES // 2, CELLS, 8, CH)
         for cell in range(CELLS):
-            patch_rows[rows, cell * CH : (cell + 1) * CH] = tiles[:, cell].reshape(256, CH).astype(BF16)
+            patch_rows[rows, cell * CH : (cell + 1) * CH] = tiles[:, cell].reshape(block, CH).astype(BF16)
         part = jnp.dot(patch_rows[rows, :], patch_weight[...], preferred_element_type=F32).astype(BF16)
-        tokens_ref[rows, :] = part
+        tokens[rows, :] = part
         values = layer_norm(part.astype(F32), gain_ref[...])
-        normed[rows, :] = values
-        normed_ref[rows, :] = values.astype(BF16)
-
-    def edge(row, col):
-        first = normed[pl.ds(pl.multiple_of(row * WP + col, 8), WIN), :]
-        second = normed[pl.ds(pl.multiple_of((row + 1) * WP + col, 8), WIN), :]
-        return jnp.concatenate([first, second], axis=0).astype(BF16)
-
-    @pl.loop(0, HP // 2, unroll=2)
-    def _(pair):
-        rows = pl.ds(pl.multiple_of(pair * 16, 16), 16)
-        west_ref[rows, :] = edge(pair * 2, 0)
-        east_ref[rows, :] = edge(pair * 2, WP - WIN)
-
-    @pl.loop(0, WIN // 2, unroll=2)
-    def _(pair):
+        normed[rows, :] = values.astype(BF16)
+        values = values.reshape(half_rows, 3, WIN, D)
+        side = slice(m * half_rows * WIN, (m + 1) * half_rows * WIN)
+        west_ref[side, :] = values[:, 0].reshape(half_rows * WIN, D).astype(BF16)
+        east_ref[side, :] = values[:, 2].reshape(half_rows * WIN, D).astype(BF16)
+        ends, target = (values[:WIN], north_ref) if m == 0 else (values[half_rows - WIN :], south_ref)
         for col in range(3):
-            rows = pl.ds(pl.multiple_of(col * WIN_TOK + pair * 16, 16), 16)
-            north_ref[rows, :] = edge(pair * 2, col * WIN)
-            south_ref[rows, :] = edge(HP - WIN + pair * 2, col * WIN)
+            target[col * WIN_TOK : (col + 1) * WIN_TOK, :] = ends[:, col].reshape(WIN_TOK, D).astype(BF16)
+        for copy in leave(m):
+            copy.start()
+
+    for m in range(2):
+        for copy in leave(m):
+            copy.wait()
 
 
 def grid_tokens(block_tiles, obs_cells, norm_gain, received, patch_weight):
     whole = lambda rows: jax.ShapeDtypeStruct((rows, D), BF16)
-    outs = [whole(n) for n in (TOKENS, TOKENS, WIN * HP, WIN * HP, WIN * WP, WIN * WP)]
+    outs = [pltpu.HBM((TOKENS, D), BF16)] * 2 + [whole(n) for n in (WIN * HP, WIN * HP, WIN * WP, WIN * WP)]
     outs.append(jax.ShapeDtypeStruct((BLOCKS, TILE), jnp.int32))
     return pl.pallas_call(
         grid_kernel,
         in_specs=[SMEM_SPEC, VMEM_SPEC, VMEM_SPEC, HBM_SPEC, HBM_SPEC],
-        out_specs=[VMEM_SPEC] * len(outs),
+        out_specs=[HBM_SPEC] * 2 + [VMEM_SPEC] * (len(outs) - 2),
         scratch_shapes=[
             pltpu.VMEM((BLOCKS, TILE, CH), BF16),
             pltpu.VMEM((TILES, TILE, CH), F32),
             pltpu.VMEM((TOKENS, CELLS * CH), BF16),
             pltpu.VMEM((CELLS * CH, D), BF16),
-            pltpu.VMEM((TOKENS, D), F32),
+            pltpu.VMEM((TOKENS, D), BF16),
+            pltpu.VMEM((TOKENS, D), BF16),
             pltpu.SemaphoreType.DMA((BLOCKS // GROUP + 1,)),
+            pltpu.SemaphoreType.DMA((4,)),
         ],
         out_shape=outs,
         compiler_params=pltpu.CompilerParams(vmem_limit_bytes=40 * MIB),
         cost_estimate=pl.CostEstimate(flops=4 * 10**9, bytes_accessed=14 * 10**6, transcendentals=0),
         name="grid_tokens",
-    )(block_tiles, obs_cells, norm_gain, received, pltpu.with_memory_space_constraint(patch_weight, pltpu.HBM))
+    )(block_tiles, obs_cells, norm_gain, received, in_hbm(patch_weight))
 
 
 INNER = (1, 1, 3, (1, 2))
@@ -270,12 +270,12 @@
 
         bias[0] = jnp.zeros((WIN_TOK, LANES), F32)
 
-    @pl.loop(0, count, unroll=count)
-    def _(step):
-        mask = bias.at[jnp.where(first + stride * step == special, 1, 0)] if edge_rows else None
+    for step in range(count):
+        row = first + stride * step
+        mask = bias.at[jnp.where(row == special, 1, 0)] if row in (0, 4) else None
 
         @pl.loop(0, D // LANES, unroll=8)
-        def _(group):
+        def _(group, step=step, mask=mask):
             for index in range(len(cols)):
                 result = attention_group(qkv, mask, ones, step * len(cols) + index, group)
                 lanes = pl.ds(pl.multiple_of(group * LANES, LANES), LANES)
@@ -290,21 +290,22 @@
     head_of_lane = lax.broadcasted_iota(jnp.int32, (WIN_TOK, LANES), 1) // HEAD
     zero = jnp.zeros((WIN_TOK, LANES), BF16)
     spread = lambda x: jnp.concatenate([jnp.where(head_of_lane == h, x, zero) for h in range(4)], axis=0)
-    scores = lax.dot_general(
-        query, spread(key), (((1,), (1,)), ((), ())), preferred_element_type=F32
-    ) * HEAD ** (-0.5)
+    scores = lax.dot_general(query, spread(key), (((1,), (1,)), ((), ())), preferred_element_type=F32)
     low = lax.broadcasted_iota(jnp.int32, (WIN_TOK, LANES), 1) < WIN_TOK
     parts = []
     for half in range(2):
         part = scores[:, half * LANES : (half + 1) * LANES]
         if mask is not None:
-            part = jnp.where(mask[...] < 0.5, part, -1000000000.0)
+            part = jnp.where(mask[...] < 0.5, part, EXCLUDED)
         low_max = jnp.max(jnp.where(low, part, -jnp.inf), axis=-1, keepdims=True)
         high_max = jnp.max(jnp.where(low, -jnp.inf, part), axis=-1, keepdims=True)
-        parts.append(jnp.exp(part - jnp.where(low, low_max, high_max)).astype(BF16))
+        parts.append(jnp.exp2((part - jnp.where(low, low_max, high_max)) * EXP_SCALE).astype(BF16))
     weights = jnp.concatenate(parts, axis=1)
     both = jnp.dot(weights, jnp.concatenate([spread(value), ones[...]], axis=1), preferred_element_type=F32)
-    return (both[:, :LANES] / both[:, LANES:]).astype(BF16).astype(F32)
+    total = both[:, LANES:]
+    inverse = pl.reciprocal(total, approx=True)
+    inverse = inverse * (2.0 - total * inverse)
+    return (both[:, :LANES] * inverse).astype(BF16).astype(F32)
 
 
 def windows_kernel(windows, *refs):
@@ -351,16 +352,17 @@
             flops=rows * D * 3 * D * 3, bytes_accessed=12 * 10**6, transcendentals=rows * 2048
         ),
         name=name,
-    )(meta, *sources, qkv_weight)
+    )(meta, *sources, in_hbm(qkv_weight))
 
 
 def tail_kernel(
-    meta_ref, tiles_ref, cells_ref, tokens_hbm, west_ref, east_ref, from_west_ref, from_east_ref,
+    meta_ref, tiles_ref, cells_ref, tokens_hbm,
+    west_ref, east_ref, from_west_ref, from_east_ref, own_west_ref, own_east_ref, west_corners_ref, east_corners_ref,
     inner_hbm, edges_hbm, out_gain_ref, read_ref, qkv_hbm, proj_hbm, unembed_hbm,
-    out_hbm,
+    out_ref,
     ext, picked, qkv, qkv_weight, bias, ones, weight_sems,
-    mixed, mixed_rows, tokens, decoded, out_stage, read_pair,
-    proj_weight, unembed_weight, in_sems, out_sems,
+    mixed, mixed_rows, tokens, decoded, read_pair,
+    proj_weight, unembed_weight, in_sems,
 ):
     row_shift, col_shift = meta_ref[0], meta_ref[1]
     inner_cols = pl.ds(WIN, 2 * WIN)
@@ -375,10 +377,14 @@
     copies = [pltpu.make_async_copy(src, dst, in_sems.at[i]) for i, (src, dst) in enumerate(moves)]
 
     def fill():
-        place(from_west_ref, 0, ext, 4 * WIN, EXT_R, 0, 0, WIN)
-        place(west_ref, 0, ext, 4 * WIN, EXT_R, 0, WIN, WIN)
-        place(east_ref, 0, ext, 4 * WIN, EXT_R, 0, 2 * WIN, WIN)
-        place(from_east_ref, 0, ext, 4 * WIN, EXT_R, 0, 3 * WIN, WIN)
+        columns = (
+            (from_west_ref, west_corners_ref), (west_ref, own_west_ref),
+            (east_ref, own_east_ref), (from_east_ref, east_corners_ref),
+        )
+        for index, (middle, ends) in enumerate(columns):
+            place(middle, 0, ext, 4 * WIN, HP, WIN, index * WIN, WIN)
+            place(ends, 0, ext, 4 * WIN, WIN, 0, index * WIN, WIN)
+            place(ends, WIN_TOK, ext, 4 * WIN, WIN, WIN + HP, index * WIN, WIN)
         read_pair[...] = jnp.zeros((2 * CH, 2 * CH), BF16)
         read_pair[:CH, :CH] = read_ref[...]
         read_pair[CH:, CH:] = read_ref[...]
@@ -436,55 +442,40 @@
 
     cell_iota = lax.broadcasted_iota(jnp.int32, (TILE, TILE), 0)
 
-    def leave(part):
-        return pltpu.make_async_copy(
-            out_stage.at[part % 2], out_hbm.at[pl.ds(part * GROUP, GROUP)], out_sems.at[part % 2]
-        )
-
     @pl.loop(0, BLOCKS // GROUP)
     def _(part):
-        @pl.when(part >= 2)
-        def _():
-            leave(part - 2).wait()
-
         for b in range(GROUP):
             block = part * GROUP + b
             cells = cells_ref[pl.ds(block, 1), :]
             one_hot = jnp.where(cell_iota == cells, 1.0, 0.0).astype(BF16)
-            out_stage[part % 2, b] = lax.dot_general(
+            out_ref[block] = lax.dot_general(
                 one_hot, decoded[tiles_ref[block]], (((0,), (0,)), ((), ())), preferred_element_type=F32
             ).astype(BF16)
-        leave(part).start()
-
-    for part in range(BLOCKS // GROUP - 2, BLOCKS // GROUP):
-        leave(part).wait()
 
 
 def tail(meta, block_tiles, live_cells, tokens, sides, mixed_parts, out_gain, read_weight, qkv_weight, proj_weight, unembed_weight):
     return pl.pallas_call(
         tail_kernel,
-        in_specs=[SMEM_SPEC, SMEM_SPEC] + [VMEM_SPEC, HBM_SPEC] + [VMEM_SPEC] * 4 + [HBM_SPEC] * 2 + [VMEM_SPEC] * 2 + [HBM_SPEC] * 3,
-        out_specs=HBM_SPEC,
-        out_shape=jax.ShapeDtypeStruct((BLOCKS, TILE, CH), BF16),
+        in_specs=[SMEM_SPEC, SMEM_SPEC] + [VMEM_SPEC, HBM_SPEC] + [VMEM_SPEC] * 8 + [HBM_SPEC] * 2 + [VMEM_SPEC] * 2 + [HBM_SPEC] * 3,
+        out_specs=VMEM_SPEC,
+        out_shape=pltpu.VMEM((BLOCKS, TILE, CH), BF16),
         scratch_shapes=attend_scratch(SIDES)
         + [
             pltpu.VMEM((SPAN_R, SPAN_C, D), F32),
             pltpu.VMEM((TOKENS, D), BF16),
             pltpu.VMEM((TOKENS, D), BF16),
             pltpu.VMEM((TILES, TILE, CH), BF16),
-            pltpu.VMEM((2, GROUP, TILE, CH), BF16),
             pltpu.VMEM((2 * CH, 2 * CH), BF16),
             pltpu.VMEM((D, D), BF16),
             pltpu.VMEM((D, 2 * D), BF16),
             pltpu.SemaphoreType.DMA((6,)),
-            pltpu.SemaphoreType.DMA((2,)),
         ],
-        compiler_params=pltpu.CompilerParams(vmem_limit_bytes=46 * MIB),
+        compiler_params=pltpu.CompilerParams(vmem_limit_bytes=40 * MIB),
         cost_estimate=pl.CostEstimate(flops=12 * 10**9, bytes_accessed=28 * 10**6, transcendentals=10**6),
         name="sides_decode",
     )(
-        meta, block_tiles, live_cells, pltpu.with_memory_space_constraint(tokens, pltpu.HBM), *sides, *mixed_parts,
-        out_gain, read_weight, qkv_weight, proj_weight, unembed_weight,
+        meta, block_tiles, live_cells, in_hbm(tokens), *sides, *mixed_parts,
+        out_gain, read_weight, in_hbm(qkv_weight), in_hbm(proj_weight), in_hbm(unembed_weight),
     )
 
 
@@ -498,15 +489,20 @@
 
 def attention_and_decode(meta, block_tiles, live_cells, tokens, normed, west, east, north, south, out_gain, read_weight, qkv_weight, proj_weight, unembed_weight):
     from_north, from_south = send(south, 0, 1), send(north, 0, -1)
-    inner = attend_windows(INNER, "inner_windows", meta, (normed,), qkv_weight)
-    from_north, from_south, inner = lax.optimization_barrier((from_north, from_south, inner))
-    west = jnp.concatenate([from_north[:WIN_TOK], west, from_south[:WIN_TOK]], axis=0)
-    east = jnp.concatenate([from_north[2 * WIN_TOK :], east, from_south[2 * WIN_TOK :]], axis=0)
     from_west, from_east = send(east, 1, 0), send(west, -1, 0)
+    inner = attend_windows(INNER, "inner_windows", meta, (in_hbm(normed),), qkv_weight)
+    from_north, from_south, from_west, from_east, inner = lax.optimization_barrier(
+        (from_north, from_south, from_west, from_east, inner)
+    )
+    first, last = slice(0, WIN_TOK), slice(2 * WIN_TOK, 3 * WIN_TOK)
+    own_west = jnp.concatenate([from_north[first], from_south[first]], axis=0)
+    own_east = jnp.concatenate([from_north[last], from_south[last]], axis=0)
+    west_corners, east_corners = send(own_east, 1, 0), send(own_west, -1, 0)
     edges = attend_windows(EDGES, "edge_windows", meta, (from_north, north, south, from_south), qkv_weight)
-    from_west, from_east, edges = lax.optimization_barrier((from_west, from_east, edges))
+    west_corners, east_corners, edges = lax.optimization_barrier((west_corners, east_corners, edges))
+    sides = (west, east, from_west, from_east, own_west, own_east, west_corners, east_corners)
     return tail(
-        meta, block_tiles, live_cells, tokens, (west, east, from_west, from_east), (inner, edges),
+        meta, block_tiles, live_cells, tokens, sides, (inner, edges),
         out_gain, read_weight, qkv_weight, proj_weight, unembed_weight,
     )
 

time: 195 us -> 188 us (0.964)
  blocking collectives: 61.4 us -> 126 us
  waiting for transfers between devices: 58.5 us -> 1.25 us
  starting transfers between devices: 16.7 us -> 6.55 us
  Pallas kernels: 54.4 us -> 52.2 us
    all_to_all x0 -> x1, blocking collectives: none -> 64.5 us  [per_device(): lax.all_to_all(outgoing, ('lon', 'lat'), split_axis=0, concat_axis=0, til...]
    all_to_all x1 -> x0, waiting for transfers between devices: 52.8 us -> none  [per_device(): lax.all_to_all(outgoing, ('lon', 'lat'), split_axis=0, concat_axis=0, til...]
    all_to_all x1 -> x0, starting transfers between devices: 12 us -> none  [per_device(): lax.all_to_all(outgoing, ('lon', 'lat'), split_axis=0, concat_axis=0, til...]
    ppermute x4 -> x6, waiting for transfers between devices: 5.66 us -> 1.25 us  [send(): return lax.ppermute(value, ('lon', 'lat'), pairs)]
    pallas_call x1, Pallas kernels: 23.2 us -> 20.7 us  [tail(): pl.pallas_call(tail_kernel, in_specs=[SMEM_SPEC, SMEM_SPEC] + [VMEM_SPEC,...]
    ppermute x4 -> x6, starting transfers between devices: 4.74 us -> 6.55 us  [send(): return lax.ppermute(value, ('lon', 'lat'), pairs)]
  transfers between devices with their start and end apart: 5 -> 6, of which waited for: 3 -> 1; matrix products, arithmetic and copies ran while one was open for 0% -> 0% of each run, Pallas kernels for 7% -> 8%
where the time goes in v1:
time: 188 us
  blocking collectives  126 us (67%)
  Pallas kernels  52.2 us (28%)
  starting transfers between devices  6.55 us (3%)
  local copies, waits for them, and re-layouts  2.09 us (1%)
    all_to_all x1, blocking collectives, per_device(): lax.all_to_all(outgoing, ('lon', 'lat'), split_axis=0, concat_axis=0, til...  64.5 us
    all_to_all x1, blocking collectives, per_device(): lax.all_to_all(sampled.reshape(BLOCKS, 1, TILE, CH), ('lon', 'lat'), spli...  61.2 us
    pallas_call x1, Pallas kernels, tail(): pl.pallas_call(tail_kernel, in_specs=[SMEM_SPEC, SMEM_SPEC] + [VMEM_SPEC,...  20.7 us
    pallas_call x2, Pallas kernels, attend_windows(): pl.pallas_call(lambda *refs: windows_kernel(windows, *refs), in_specs=[SM...  14.3 us
    pallas_call x1, Pallas kernels, grid_tokens(): pl.pallas_call(grid_kernel, in_specs=[SMEM_SPEC, VMEM_SPEC, VMEM_SPEC, HB...  10.2 us
    pallas_call x1, Pallas kernels, embed(): pl.pallas_call(embed_kernel, in_specs=[SMEM_SPEC, VMEM_SPEC, VMEM_SPEC, H...  7.05 us
    ppermute x6, starting transfers between devices, send(): return lax.ppermute(value, ('lon', 'lat'), pairs)  6.55 us
  transfers between devices with their start and end apart: 6, of which 1 were waited for; matrix products, arithmetic and copies ran while one was open for 0% of the time, Pallas kernels for 8%

profile of v1, /device:TPU:1, one launch (start us, length us, event | category | flops | bytes accessed | tf_op | source)
XLA Modules:
  0.0 188.0 jit_solution(15045944408227253847)
XLA Ops:
  0.0 7.0 %embed.1 = bf16[128,128,128]{2,1,0:T(8,128)(2,1)S(1)} custom-call(s32[128]{0:T(128)} %bitcast.25, f32[128,128]{1,0:T(8,128)} %bitcast.24, bf16[128,128]{1,0:T(8,128)(2,1)} %embed_ref.1, bf16[128,128,128]{2,1,0:T(8,128)(2,1)} %bitcast.23), custom_call_target="tpu_custom_call" | custom-call | flops 600000000 | bytes 8000000 | tf_op jit(solution)/shard_map/embed/pallas_call | solution.py:76
  7.1 0.0 copy-start
  7.1 0.0 copy-start.2
  7.1 0.0 copy-start.4
  7.1 64.5 %all_to_all.10 = bf16[128,1,128,128]{3,2,1,0:T(8,128)(2,1)S(1)} all-to-all(bf16[128,1,128,128]{3,2,1,0:T(8,128)(2,1)S(1)} %bitcast.15), channel_id=1, replica_groups=mesh['lon'=32,'lat'=4] {'lon','lat'}, dimensions={0} | all-to-all | bytes 8388608 | tf_op jit(solution)/shard_map/all_to_all | solution.py:529
  71.6 0.0 copy-start.5
  71.6 10.2 %grid_tokens.1 = (bf16[768,1024]{1,0:T(8,128)(2,1)}, bf16[768,1024]{1,0:T(8,128)(2,1)}, bf16[256,1024]{1,0:T(8,128)(2,1)S(1)}, bf16[256,1024]{1,0:T(8,128)(2,1)S...) custom-call(s32[128]{0:T(128)S(1)} %bitcast.21, ...), custom_call_target="tpu_custom_call" | custom-call | flops 4000000000 | bytes 14000000 | tf_op jit(solution)/shard_map/grid_tokens/pallas_call | solution.py:172
  81.9 0.1 collective-permute-start.3
  81.9 1.7 collective-permute-start.2
  83.7 0.3 collective-permute-start
  84.0 2.3 %collective-permute-start.1 = (bf16[192,1024]{1,0:T(8,128)(2,1)S(1)}, bf16[192,1024]{1,0:T(8,128)(2,1)S(1)}, u32[]{:S(2)}, u32[]{:S(2)}) collective-permute-start(bf16[192,1024]{1,0:T(8,128)(2,1)S(1)} %get-tuple-element.25.refs_2_), channel_id=1, source_target_pairs={{0,3},{1,0},{2,1},{3,2},{4,7},{5,4},{6,5},{7,6},{8,11},{9,8},{10,9... | collective-permute-start | bytes 1179656 | tf_op jit(solution)/shard_map/ppermute | solution.py:487
  86.4 0.1 pad_add_fusion.refs_0_.meta_ref
  86.4 8.3 %inner_windows.1.inner_hbm = f32[24,16,1024]{2,1,0:T(8,128)S(1)} custom-call(s32[3]{0:T(128)S(1)} %pad_add_fusion.refs_0_.meta_ref, bf16[768,1024]{1,0:T(8,128)(2,1)} %get-tuple-element.26.refs_1_, bf16[1024,3072]{1,0:T(8,128)(2,1)} %qkv_hbm.1), custom_call_target="tpu_custom_call" | custom-call | flops 3623878656 | bytes 12000000 | tf_op jit(solution)/shard_map/inner_windows/pallas_call | solution.py:344
  94.7 1.2 collective-permute-done.refs_1_
  96.0 0.0 collective-permute-done.1.refs_4_
  96.0 0.0 collective-permute-done.3.from_east_ref
  96.1 0.5 collective-permute-start.5
  96.5 0.0 copy-start.1
  96.5 0.0 copy-start.3
  96.6 1.6 collective-permute-start.4
  98.2 6.0 %edge_windows.1.edges_hbm = f32[16,16,1024]{2,1,0:T(8,128)S(1)} custom-call(s32[3]{0:T(128)S(1)} %pad_add_fusion.refs_0_.meta_ref, bf16[192,1024]{1,0:T(8,128)(2,1)S(1)} %collective-permute-done.refs_1_, bf16[192,1024]{1,0:T(8,128)(2,1)S(1)} %get-tuple-element.25.refs_2_, bf16[192,1024]{1,0:T(8,128)(2,1)S(1)} %get-tuple-element.24.refs_3_, ...), custom_call_target="tpu_custom_call" | custom-call | flops 2415919104 | bytes 12000000 | tf_op jit(solution)/shard_map/edge_windows/pallas_call | solution.py:344
  104.2 20.7 %sides_decode.1 = bf16[128,128,128]{2,1,0:T(8,128)(2,1)S(1)} custom-call(s32[3]{0:T(128)S(1)} %pad_add_fusion.refs_0_.meta_ref, s32[128]{0:T(128)S(1)} %bitcast.22, s32[128,128]{1,0:T(8,128)S(1)} %get-tuple-element.20.cells_ref, bf16[768,1024]{1,0:T(8,128)(2,1)} %get-tuple-element.21.tokens_hbm, bf16[256,1024]{1,0:T(8,128)(2,1)S(1)} %get-tuple-element.22.west_ref, ...), custom_call_target="tpu_custom_call" | custom-call | flops 12000000000 | bytes 28000000 | tf_op jit(solution)/shard_map/sides_decode/pallas_call | solution.py:457
  124.9 61.2 %all_to_all.11 = bf16[128,1,128,128]{3,2,1,0:T(8,128)(2,1)S(1)} all-to-all(bf16[128,1,128,128]{3,2,1,0:T(8,128)(2,1)S(1)} %bitcast.16), channel_id=1, replica_groups=mesh['lon'=32,'lat'=4] {'lon','lat'}, dimensions={0} | all-to-all | bytes 8388608 | tf_op jit(solution)/shard_map/all_to_all | solution.py:543
  186.0 2.0 %copy.19 = bf16[128,1,128,128]{3,2,1,0:T(8,128)(2,1)} copy(bf16[128,1,128,128]{3,2,1,0:T(8,128)(2,1)S(1)} %all_to_all.11) | data formatting | bytes 8388608
  (12 shorter events, 0.1 us)
Async XLA Ops:
  7.1 64.6 %copy-start = (s32[128,1,128]{2,1,0:T(1,128)S(1)}, s32[128,1,128]{2,1,0:T(1,128)}, u32[]{:S(2)}) copy-start(s32[128,1,128]{2,1,0:T(1,128)} %param.17) | copy-start | bytes 196612
  7.1 64.5 %copy-start.2 = (f32[1024]{0:T(1024)S(1)}, f32[1024]{0:T(1024)}, u32[]{:S(2)}) copy-start(f32[1024]{0:T(1024)} %param.22) | copy-start | bytes 12292
  7.1 64.5 %copy-start.4 = (s32[128,1]{0,1:T(1,128)S(1)}, s32[128,1]{0,1:T(1,128)}, u32[]{:S(2)}) copy-start(s32[128,1]{0,1:T(1,128)} %param.18) | copy-start | bytes 1540
  71.6 14.7 %copy-start.5 = (s32[2]{0:T(128)S(1)}, s32[2]{0:T(128)}, u32[]{:S(2)}) copy-start(s32[2]{0:T(128)} %param.19) | copy-start | bytes 28
  81.9 14.1 %collective-permute-start.3 = (bf16[256,1024]{1,0:T(8,128)(2,1)S(1)}, bf16[256,1024]{1,0:T(8,128)(2,1)S(1)}, u32[]{:S(2)}, u32[]{:S(2)}) collective-permute-start(bf16[256,1024]{1,0:T(8,128)(2,1)S(1)} %get-tuple-element.22.west_ref), channel_id=1, source_target_pairs={{0,124},{1,125},{2,126},{3,127},{4,0},{5,1},{6,2},{7,3},{8,4},{9,5... | collective-permute-start | bytes 1572872 | tf_op jit(solution)/shard_map/ppermute | solution.py:487
  81.9 14.0 %collective-permute-start.2 = (bf16[256,1024]{1,0:T(8,128)(2,1)S(1)}, bf16[256,1024]{1,0:T(8,128)(2,1)S(1)}, u32[]{:S(2)}, u32[]{:S(2)}) collective-permute-start(bf16[256,1024]{1,0:T(8,128)(2,1)S(1)} %get-tuple-element.23.east_ref), channel_id=1, source_target_pairs={{0,4},{1,5},{2,6},{3,7},{4,8},{5,9},{6,10},{7,11},{8,12},{9,13},{1... | collective-permute-start | bytes 1572872 | tf_op jit(solution)/shard_map/ppermute | solution.py:487
  83.7 12.3 %collective-permute-start = (bf16[192,1024]{1,0:T(8,128)(2,1)S(1)}, bf16[192,1024]{1,0:T(8,128)(2,1)S(1)}, u32[]{:S(2)}, u32[]{:S(2)}) collective-permute-start(bf16[192,1024]{1,0:T(8,128)(2,1)S(1)} %get-tuple-element.24.refs_3_), channel_id=1, source_target_pairs={{0,1},{1,2},{2,3},{3,0},{4,5},{5,6},{6,7},{7,4},{8,9},{9,10},{10,1... | collective-permute-start | bytes 1179656 | tf_op jit(solution)/shard_map/ppermute | solution.py:487
  84.0 11.9 %collective-permute-start.1 = (bf16[192,1024]{1,0:T(8,128)(2,1)S(1)}, bf16[192,1024]{1,0:T(8,128)(2,1)S(1)}, u32[]{:S(2)}, u32[]{:S(2)}) collective-permute-start(bf16[192,1024]{1,0:T(8,128)(2,1)S(1)} %get-tuple-element.25.refs_2_), channel_id=1, source_target_pairs={{0,3},{1,0},{2,1},{3,2},{4,7},{5,4},{6,5},{7,6},{8,11},{9,8},{10,9... | collective-permute-start | bytes 1179656 | tf_op jit(solution)/shard_map/ppermute | solution.py:487
  96.1 8.1 %collective-permute-start.5 = (bf16[128,1024]{1,0:T(8,128)(2,1)S(1)}, bf16[128,1024]{1,0:T(8,128)(2,1)S(1)}, u32[]{:S(2)}, u32[]{:S(2)}) collective-permute-start(bf16[128,1024]{1,0:T(8,128)(2,1)S(1)} %pad_maximum_fusion.own_west_ref), channel_id=1, source_target_pairs={{0,124},{1,125},{2,126},{3,127},{4,0},{5,1},{6,2},{7,3},{8,4},{9,5... | collective-permute-start | bytes 786440 | tf_op jit(solution)/shard_map/ppermute | solution.py:487
  96.5 7.6 %copy-start.1 = (bf16[128,128]{1,0:T(8,128)(2,1)S(1)}, bf16[128,128]{1,0:T(8,128)(2,1)}, u32[]{:S(2)}) copy-start(bf16[128,128]{1,0:T(8,128)(2,1)} %read_ref.1) | copy-start | bytes 98308
  96.5 7.6 %copy-start.3 = (f32[1024]{0:T(1024)S(1)}, f32[1024]{0:T(1024)}, u32[]{:S(2)}) copy-start(f32[1024]{0:T(1024)} %param.25) | copy-start | bytes 12292
  96.6 7.6 %collective-permute-start.4 = (bf16[128,1024]{1,0:T(8,128)(2,1)S(1)}, bf16[128,1024]{1,0:T(8,128)(2,1)S(1)}, u32[]{:S(2)}, u32[]{:S(2)}) collective-permute-start(bf16[128,1024]{1,0:T(8,128)(2,1)S(1)} %pad_maximum_fusion.1.own_east_ref), channel_id=1, source_target_pairs={{0,4},{1,5},{2,6},{3,7},{4,8},{5,9},{6,10},{7,11},{8,12},{9,13},{1... | collective-permute-start | bytes 786440 | tf_op jit(solution)/shard_map/ppermute | solution.py:487

commit v2 on v1

--- a/solution.py
+++ b/solution.py
@@ -42,6 +42,10 @@
     return pltpu.with_memory_space_constraint(value, pltpu.HBM)
 
 
+def in_vmem(value):
+    return pltpu.with_memory_space_constraint(value, pltpu.VMEM)
+
+
 def layer_norm(values, gain_vector):
     row_mean = jnp.mean(values, axis=-1, keepdims=True)
     centered = values - row_mean
@@ -60,7 +64,7 @@
         arrival(part).start()
     slot_iota = lax.broadcasted_iota(jnp.int32, (TILE, CH), 0)
 
-    @pl.loop(0, parts)
+    @pl.loop(0, parts, unroll=4)
     def _(part):
         first = pl.multiple_of(part * GROUP, GROUP)
         columns = (weights_ref[pl.ds(first, GROUP), :] * 0.5).T
@@ -89,19 +93,12 @@
 
 
 def grid_kernel(
-    tiles_ref, cells_ref, gain_ref, received_hbm, patch_hbm,
+    tiles_ref, cells_ref, gain_ref, received, patch_hbm,
     tokens_hbm, normed_hbm, west_ref, east_ref, north_ref, south_ref, live_cells_ref,
-    received, cell_sums, patch_rows, patch_weight, tokens, normed, sems, out_sems,
+    cell_sums, patch_rows, patch_weight, tokens, normed, weight_sem, out_sems,
 ):
     parts = BLOCKS // GROUP
-
-    def arrival(part):
-        rows = pl.ds(part * GROUP, GROUP)
-        return pltpu.make_async_copy(received_hbm.at[rows], received.at[rows], sems.at[part])
-
-    for part in range(parts):
-        arrival(part).start()
-    weight_copy = pltpu.make_async_copy(patch_hbm, patch_weight, sems.at[parts])
+    weight_copy = pltpu.make_async_copy(patch_hbm, patch_weight, weight_sem)
     weight_copy.start()
 
     @pl.loop(0, TILES, unroll=2)
@@ -111,9 +108,8 @@
     cell_iota = lax.broadcasted_iota(jnp.int32, (TILE, TILE), 0)
     slot_iota = lax.broadcasted_iota(jnp.int32, (1, TILE), 1).astype(F32)
 
-    @pl.loop(0, parts)
+    @pl.loop(0, parts, unroll=4)
     def _(part):
-        arrival(part).wait()
         first = pl.multiple_of(part * GROUP, GROUP)
         all_cells = cells_ref[pl.ds(first, GROUP), :]
         all_cells = (all_cells & 15) * 8 + (all_cells >> 4)
@@ -171,23 +167,22 @@
     outs.append(jax.ShapeDtypeStruct((BLOCKS, TILE), jnp.int32))
     return pl.pallas_call(
         grid_kernel,
-        in_specs=[SMEM_SPEC, VMEM_SPEC, VMEM_SPEC, HBM_SPEC, HBM_SPEC],
+        in_specs=[SMEM_SPEC, VMEM_SPEC, VMEM_SPEC, VMEM_SPEC, HBM_SPEC],
         out_specs=[HBM_SPEC] * 2 + [VMEM_SPEC] * (len(outs) - 2),
         scratch_shapes=[
-            pltpu.VMEM((BLOCKS, TILE, CH), BF16),
             pltpu.VMEM((TILES, TILE, CH), F32),
             pltpu.VMEM((TOKENS, CELLS * CH), BF16),
             pltpu.VMEM((CELLS * CH, D), BF16),
             pltpu.VMEM((TOKENS, D), BF16),
             pltpu.VMEM((TOKENS, D), BF16),
-            pltpu.SemaphoreType.DMA((BLOCKS // GROUP + 1,)),
+            pltpu.SemaphoreType.DMA,
             pltpu.SemaphoreType.DMA((4,)),
         ],
         out_shape=outs,
-        compiler_params=pltpu.CompilerParams(vmem_limit_bytes=40 * MIB),
+        compiler_params=pltpu.CompilerParams(vmem_limit_bytes=32 * MIB),
         cost_estimate=pl.CostEstimate(flops=4 * 10**9, bytes_accessed=14 * 10**6, transcendentals=0),
         name="grid_tokens",
-    )(block_tiles, obs_cells, norm_gain, received, in_hbm(patch_weight))
+    )(block_tiles, obs_cells, norm_gain, in_vmem(received), in_hbm(patch_weight))
 
 
 INNER = (1, 1, 3, (1, 2))
@@ -442,7 +437,7 @@
 
     cell_iota = lax.broadcasted_iota(jnp.int32, (TILE, TILE), 0)
 
-    @pl.loop(0, BLOCKS // GROUP)
+    @pl.loop(0, BLOCKS // GROUP, unroll=2)
     def _(part):
         for b in range(GROUP):
             block = part * GROUP + b

time: 188 us -> 186 us (0.989)
  Pallas kernels: 52.2 us -> 50.3 us
where the time goes in v2:
time: 186 us
  blocking collectives  126 us (68%)
  Pallas kernels  50.3 us (27%)
  starting transfers between devices  6.37 us (3%)
  local copies, waits for them, and re-layouts  2.09 us (1%)
    all_to_all x1, blocking collectives, per_device(): lax.all_to_all(outgoing, ('lon', 'lat'), split_axis=0, concat_axis=0, til...  64.5 us
    all_to_all x1, blocking collectives, per_device(): lax.all_to_all(sampled.reshape(BLOCKS, 1, TILE, CH), ('lon', 'lat'), spli...  61.2 us
    pallas_call x1, Pallas kernels, tail(): pl.pallas_call(tail_kernel, in_specs=[SMEM_SPEC, SMEM_SPEC] + [VMEM_SPEC,...  19.9 us
    pallas_call x2, Pallas kernels, attend_windows(): pl.pallas_call(lambda *refs: windows_kernel(windows, *refs), in_specs=[SM...  14.3 us
    pallas_call x1, Pallas kernels, grid_tokens(): pl.pallas_call(grid_kernel, in_specs=[SMEM_SPEC, VMEM_SPEC, VMEM_SPEC, VM...  9.43 us
    pallas_call x1, Pallas kernels, embed(): pl.pallas_call(embed_kernel, in_specs=[SMEM_SPEC, VMEM_SPEC, VMEM_SPEC, H...  6.72 us
    ppermute x6, starting transfers between devices, send(): return lax.ppermute(value, ('lon', 'lat'), pairs)  6.37 us
  transfers between devices with their start and end apart: 6, of which 1 were waited for; matrix products, arithmetic and copies ran while one was open for 0% of the time, Pallas kernels for 8%

profile of v2, /device:TPU:1, one launch (start us, length us, event | category | flops | bytes accessed | tf_op | source)
XLA Modules:
  0.0 186.0 jit_solution(12609221271383743826)
XLA Ops:
  0.0 6.7 %embed.1 = bf16[128,128,128]{2,1,0:T(8,128)(2,1)S(1)} custom-call(s32[128]{0:T(128)} %bitcast.25, f32[128,128]{1,0:T(8,128)} %bitcast.24, bf16[128,128]{1,0:T(8,128)(2,1)} %embed_ref.1, bf16[128,128,128]{2,1,0:T(8,128)(2,1)} %bitcast.23), custom_call_target="tpu_custom_call" | custom-call | flops 600000000 | bytes 8000000 | tf_op jit(solution)/shard_map/embed/pallas_call | solution.py:80
  6.7 0.0 copy-start
  6.7 0.0 copy-start.2
  6.8 0.0 copy-start.4
  6.8 64.5 %all_to_all.10 = bf16[128,1,128,128]{3,2,1,0:T(8,128)(2,1)S(1)} all-to-all(bf16[128,1,128,128]{3,2,1,0:T(8,128)(2,1)S(1)} %bitcast.15), channel_id=1, replica_groups=mesh['lon'=32,'lat'=4] {'lon','lat'}, dimensions={0} | all-to-all | bytes 8388608 | tf_op jit(solution)/shard_map/all_to_all | solution.py:524
  71.3 0.0 copy-start.5
  71.3 9.4 %grid_tokens.1 = (bf16[768,1024]{1,0:T(8,128)(2,1)}, bf16[768,1024]{1,0:T(8,128)(2,1)}, bf16[256,1024]{1,0:T(8,128)(2,1)S(1)}, bf16[256,1024]{1,0:T(8,128)(2,1)S...) custom-call(s32[128]{0:T(128)S(1)} %bitcast.21, ...), custom_call_target="tpu_custom_call" | custom-call | flops 4000000000 | bytes 14000000 | tf_op jit(solution)/shard_map/grid_tokens/pallas_call | solution.py:168
  80.7 0.1 collective-permute-start.3
  80.8 1.7 collective-permute-start.2
  82.6 0.4 collective-permute-start
  82.9 2.3 %collective-permute-start.1 = (bf16[192,1024]{1,0:T(8,128)(2,1)S(1)}, bf16[192,1024]{1,0:T(8,128)(2,1)S(1)}, u32[]{:S(2)}, u32[]{:S(2)}) collective-permute-start(bf16[192,1024]{1,0:T(8,128)(2,1)S(1)} %get-tuple-element.25.refs_2_), channel_id=1, source_target_pairs={{0,3},{1,0},{2,1},{3,2},{4,7},{5,4},{6,5},{7,6},{8,11},{9,8},{10,9... | collective-permute-start | bytes 1179656 | tf_op jit(solution)/shard_map/ppermute | solution.py:482
  85.2 0.1 pad_add_fusion.refs_0_.meta_ref
  85.3 8.3 %inner_windows.1.inner_hbm = f32[24,16,1024]{2,1,0:T(8,128)S(1)} custom-call(s32[3]{0:T(128)S(1)} %pad_add_fusion.refs_0_.meta_ref, bf16[768,1024]{1,0:T(8,128)(2,1)} %get-tuple-element.26.refs_1_, bf16[1024,3072]{1,0:T(8,128)(2,1)} %qkv_hbm.1), custom_call_target="tpu_custom_call" | custom-call | flops 3623878656 | bytes 12000000 | tf_op jit(solution)/shard_map/inner_windows/pallas_call | solution.py:339
  93.6 1.2 collective-permute-done.refs_1_
  94.9 0.0 collective-permute-done.1.refs_4_
  94.9 0.5 collective-permute-start.5
  95.4 0.0 copy-start.1
  95.4 0.0 copy-start.3
  95.4 1.4 collective-permute-start.4
  96.9 6.0 %edge_windows.1.edges_hbm = f32[16,16,1024]{2,1,0:T(8,128)S(1)} custom-call(s32[3]{0:T(128)S(1)} %pad_add_fusion.refs_0_.meta_ref, bf16[192,1024]{1,0:T(8,128)(2,1)S(1)} %collective-permute-done.refs_1_, bf16[192,1024]{1,0:T(8,128)(2,1)S(1)} %get-tuple-element.25.refs_2_, bf16[192,1024]{1,0:T(8,128)(2,1)S(1)} %get-tuple-element.24.refs_3_, ...), custom_call_target="tpu_custom_call" | custom-call | flops 2415919104 | bytes 12000000 | tf_op jit(solution)/shard_map/edge_windows/pallas_call | solution.py:339
  102.8 0.0 collective-permute-done.5.east_corners_ref
  102.9 19.9 %sides_decode.1 = bf16[128,128,128]{2,1,0:T(8,128)(2,1)S(1)} custom-call(s32[3]{0:T(128)S(1)} %pad_add_fusion.refs_0_.meta_ref, s32[128]{0:T(128)S(1)} %bitcast.22, s32[128,128]{1,0:T(8,128)S(1)} %get-tuple-element.20.cells_ref, bf16[768,1024]{1,0:T(8,128)(2,1)} %get-tuple-element.21.tokens_hbm, bf16[256,1024]{1,0:T(8,128)(2,1)S(1)} %get-tuple-element.22.west_ref, ...), custom_call_target="tpu_custom_call" | custom-call | flops 12000000000 | bytes 28000000 | tf_op jit(solution)/shard_map/sides_decode/pallas_call | solution.py:452
  122.8 61.2 %all_to_all.11 = bf16[128,1,128,128]{3,2,1,0:T(8,128)(2,1)S(1)} all-to-all(bf16[128,1,128,128]{3,2,1,0:T(8,128)(2,1)S(1)} %bitcast.16), channel_id=1, replica_groups=mesh['lon'=32,'lat'=4] {'lon','lat'}, dimensions={0} | all-to-all | bytes 8388608 | tf_op jit(solution)/shard_map/all_to_all | solution.py:538
  183.9 2.0 %copy.19 = bf16[128,1,128,128]{3,2,1,0:T(8,128)(2,1)} copy(bf16[128,1,128,128]{3,2,1,0:T(8,128)(2,1)S(1)} %all_to_all.11) | data formatting | bytes 8388608
  (12 shorter events, 0.1 us)
Async XLA Ops:
  6.7 64.6 %copy-start = (s32[128,1,128]{2,1,0:T(1,128)S(1)}, s32[128,1,128]{2,1,0:T(1,128)}, u32[]{:S(2)}) copy-start(s32[128,1,128]{2,1,0:T(1,128)} %param.17) | copy-start | bytes 196612
  6.7 64.5 %copy-start.2 = (f32[1024]{0:T(1024)S(1)}, f32[1024]{0:T(1024)}, u32[]{:S(2)}) copy-start(f32[1024]{0:T(1024)} %param.22) | copy-start | bytes 12292
  6.8 64.5 %copy-start.4 = (s32[128,1]{0,1:T(1,128)S(1)}, s32[128,1]{0,1:T(1,128)}, u32[]{:S(2)}) copy-start(s32[128,1]{0,1:T(1,128)} %param.18) | copy-start | bytes 1540
  71.3 13.9 %copy-start.5 = (s32[2]{0:T(128)S(1)}, s32[2]{0:T(128)}, u32[]{:S(2)}) copy-start(s32[2]{0:T(128)} %param.19) | copy-start | bytes 28
  80.7 14.1 %collective-permute-start.3 = (bf16[256,1024]{1,0:T(8,128)(2,1)S(1)}, bf16[256,1024]{1,0:T(8,128)(2,1)S(1)}, u32[]{:S(2)}, u32[]{:S(2)}) collective-permute-start(bf16[256,1024]{1,0:T(8,128)(2,1)S(1)} %get-tuple-element.22.west_ref), channel_id=1, source_target_pairs={{0,124},{1,125},{2,126},{3,127},{4,0},{5,1},{6,2},{7,3},{8,4},{9,5... | collective-permute-start | bytes 1572872 | tf_op jit(solution)/shard_map/ppermute | solution.py:482
  80.8 14.0 %collective-permute-start.2 = (bf16[256,1024]{1,0:T(8,128)(2,1)S(1)}, bf16[256,1024]{1,0:T(8,128)(2,1)S(1)}, u32[]{:S(2)}, u32[]{:S(2)}) collective-permute-start(bf16[256,1024]{1,0:T(8,128)(2,1)S(1)} %get-tuple-element.23.east_ref), channel_id=1, source_target_pairs={{0,4},{1,5},{2,6},{3,7},{4,8},{5,9},{6,10},{7,11},{8,12},{9,13},{1... | collective-permute-start | bytes 1572872 | tf_op jit(solution)/shard_map/ppermute | solution.py:482
  82.6 12.3 %collective-permute-start = (bf16[192,1024]{1,0:T(8,128)(2,1)S(1)}, bf16[192,1024]{1,0:T(8,128)(2,1)S(1)}, u32[]{:S(2)}, u32[]{:S(2)}) collective-permute-start(bf16[192,1024]{1,0:T(8,128)(2,1)S(1)} %get-tuple-element.24.refs_3_), channel_id=1, source_target_pairs={{0,1},{1,2},{2,3},{3,0},{4,5},{5,6},{6,7},{7,4},{8,9},{9,10},{10,1... | collective-permute-start | bytes 1179656 | tf_op jit(solution)/shard_map/ppermute | solution.py:482
  82.9 11.9 %collective-permute-start.1 = (bf16[192,1024]{1,0:T(8,128)(2,1)S(1)}, bf16[192,1024]{1,0:T(8,128)(2,1)S(1)}, u32[]{:S(2)}, u32[]{:S(2)}) collective-permute-start(bf16[192,1024]{1,0:T(8,128)(2,1)S(1)} %get-tuple-element.25.refs_2_), channel_id=1, source_target_pairs={{0,3},{1,0},{2,1},{3,2},{4,7},{5,4},{6,5},{7,6},{8,11},{9,8},{10,9... | collective-permute-start | bytes 1179656 | tf_op jit(solution)/shard_map/ppermute | solution.py:482
  94.9 7.9 %collective-permute-start.5 = (bf16[128,1024]{1,0:T(8,128)(2,1)S(1)}, bf16[128,1024]{1,0:T(8,128)(2,1)S(1)}, u32[]{:S(2)}, u32[]{:S(2)}) collective-permute-start(bf16[128,1024]{1,0:T(8,128)(2,1)S(1)} %pad_maximum_fusion.own_west_ref), channel_id=1, source_target_pairs={{0,124},{1,125},{2,126},{3,127},{4,0},{5,1},{6,2},{7,3},{8,4},{9,5... | collective-permute-start | bytes 786440 | tf_op jit(solution)/shard_map/ppermute | solution.py:482
  95.4 7.4 %copy-start.1 = (bf16[128,128]{1,0:T(8,128)(2,1)S(1)}, bf16[128,128]{1,0:T(8,128)(2,1)}, u32[]{:S(2)}) copy-start(bf16[128,128]{1,0:T(8,128)(2,1)} %read_ref.1) | copy-start | bytes 98308
  95.4 7.4 %copy-start.3 = (f32[1024]{0:T(1024)S(1)}, f32[1024]{0:T(1024)}, u32[]{:S(2)}) copy-start(f32[1024]{0:T(1024)} %param.25) | copy-start | bytes 12292
  95.4 7.4 %collective-permute-start.4 = (bf16[128,1024]{1,0:T(8,128)(2,1)S(1)}, bf16[128,1024]{1,0:T(8,128)(2,1)S(1)}, u32[]{:S(2)}, u32[]{:S(2)}) collective-permute-start(bf16[128,1024]{1,0:T(8,128)(2,1)S(1)} %pad_maximum_fusion.1.own_east_ref), channel_id=1, source_target_pairs={{0,4},{1,5},{2,6},{3,7},{4,8},{5,9},{6,10},{7,11},{8,12},{9,13},{1... | collective-permute-start | bytes 786440 | tf_op jit(solution)/shard_map/ppermute | solution.py:482

commit v3 on v2

--- a/solution.py
+++ b/solution.py
@@ -304,11 +304,23 @@
 
 
 def windows_kernel(windows, *refs):
+    if windows is INNER:
+        *refs, normed, normed_sems = refs
     meta_ref, *sources, qkv_hbm, out, ext, picked, qkv, qkv_weight, bias, ones, weight_sems = refs
+
+    def arrival(half):
+        rows = pl.ds(half * (TOKENS // 2), TOKENS // 2)
+        return pltpu.make_async_copy(sources[0].at[rows], normed.at[rows], normed_sems.at[half])
+
+    if windows is INNER:
+        for half in range(2):
+            arrival(half).start()
 
     def fill():
         if windows is INNER:
-            place(sources[0], 0, ext, WP, HP, 0, 0, WP)
+            for half in range(2):
+                arrival(half).wait()
+                place(normed, half * (TOKENS // 2), ext, WP, HP // 2, half * (HP // 2), 0, WP)
             return WIN
         for index, source in enumerate(sources):
             for col in range(3):
@@ -338,10 +350,11 @@
     rows = slots_of(windows) * WIN_TOK
     return pl.pallas_call(
         lambda *refs: windows_kernel(windows, *refs),
-        in_specs=[SMEM_SPEC] + [VMEM_SPEC] * len(sources) + [HBM_SPEC],
+        in_specs=[SMEM_SPEC] + [HBM_SPEC if windows is INNER else VMEM_SPEC] * len(sources) + [HBM_SPEC],
         out_specs=VMEM_SPEC,
         out_shape=jax.ShapeDtypeStruct((windows[2] * WIN, 2 * WIN, D), F32),
-        scratch_shapes=attend_scratch(windows),
+        scratch_shapes=attend_scratch(windows)
+        + ([pltpu.VMEM((TOKENS, D), BF16), pltpu.SemaphoreType.DMA((2,))] if windows is INNER else []),
         compiler_params=pltpu.CompilerParams(vmem_limit_bytes=28 * MIB),
         cost_estimate=pl.CostEstimate(
             flops=rows * D * 3 * D * 3, bytes_accessed=12 * 10**6, transcendentals=rows * 2048

time: 186 us -> 187 us (level)
  no operation moved by 1% of the time
where the time goes in v3:
time: 187 us; the launch traced here: 186 us
  blocking collectives  126 us (67%)
  Pallas kernels  51 us (27%)
  starting transfers between devices  6.37 us (3%)
  local copies, waits for them, and re-layouts  2.09 us (1%)
    all_to_all x1, blocking collectives, per_device(): lax.all_to_all(outgoing, ('lon', 'lat'), split_axis=0, concat_axis=0, til...  64.5 us
    all_to_all x1, blocking collectives, per_device(): lax.all_to_all(sampled.reshape(BLOCKS, 1, TILE, CH), ('lon', 'lat'), spli...  61.6 us
    pallas_call x1, Pallas kernels, tail(): pl.pallas_call(tail_kernel, in_specs=[SMEM_SPEC, SMEM_SPEC] + [VMEM_SPEC,...  19.9 us
    pallas_call x2, Pallas kernels, attend_windows(): pl.pallas_call(lambda *refs: windows_kernel(windows, *refs), in_specs=[SM...  15 us
    pallas_call x1, Pallas kernels, grid_tokens(): pl.pallas_call(grid_kernel, in_specs=[SMEM_SPEC, VMEM_SPEC, VMEM_SPEC, VM...  9.43 us
    pallas_call x1, Pallas kernels, embed(): pl.pallas_call(embed_kernel, in_specs=[SMEM_SPEC, VMEM_SPEC, VMEM_SPEC, H...  6.72 us
    ppermute x6, starting transfers between devices, send(): return lax.ppermute(value, ('lon', 'lat'), pairs)  6.37 us
  transfers between devices with their start and end apart: 6, of which 1 were waited for; matrix products, arithmetic and copies ran while one was open for 0% of the time, Pallas kernels for 8%

profile of v3, /device:TPU:1, one launch (start us, length us, event | category | flops | bytes accessed | tf_op | source)
XLA Modules:
  0.0 186.4 jit_solution(377489303717497373)
XLA Ops:
  0.0 6.7 %embed.1 = bf16[128,128,128]{2,1,0:T(8,128)(2,1)S(1)} custom-call(s32[128]{0:T(128)} %bitcast.25, f32[128,128]{1,0:T(8,128)} %bitcast.24, bf16[128,128]{1,0:T(8,128)(2,1)} %embed_ref.1, bf16[128,128,128]{2,1,0:T(8,128)(2,1)} %bitcast.23), custom_call_target="tpu_custom_call" | custom-call | flops 600000000 | bytes 8000000 | tf_op jit(solution)/shard_map/embed/pallas_call | solution.py:80
  6.7 0.0 copy-start
  6.7 0.0 copy-start.2
  6.8 0.0 copy-start.4
  6.8 64.5 %all_to_all.10 = bf16[128,1,128,128]{3,2,1,0:T(8,128)(2,1)S(1)} all-to-all(bf16[128,1,128,128]{3,2,1,0:T(8,128)(2,1)S(1)} %bitcast.15), channel_id=1, replica_groups=mesh['lon'=32,'lat'=4] {'lon','lat'}, dimensions={0} | all-to-all | bytes 8388608 | tf_op jit(solution)/shard_map/all_to_all | solution.py:537
  71.3 0.0 copy-start.5
  71.3 9.4 %grid_tokens.1 = (bf16[768,1024]{1,0:T(8,128)(2,1)}, bf16[768,1024]{1,0:T(8,128)(2,1)}, bf16[256,1024]{1,0:T(8,128)(2,1)S(1)}, bf16[256,1024]{1,0:T(8,128)(2,1)S...) custom-call(s32[128]{0:T(128)S(1)} %bitcast.21, ...), custom_call_target="tpu_custom_call" | custom-call | flops 4000000000 | bytes 14000000 | tf_op jit(solution)/shard_map/grid_tokens/pallas_call | solution.py:168
  80.7 0.1 collective-permute-start.3
  80.8 1.7 collective-permute-start.2
  82.6 0.4 collective-permute-start
  82.9 2.3 %collective-permute-start.1 = (bf16[192,1024]{1,0:T(8,128)(2,1)S(1)}, bf16[192,1024]{1,0:T(8,128)(2,1)S(1)}, u32[]{:S(2)}, u32[]{:S(2)}) collective-permute-start(bf16[192,1024]{1,0:T(8,128)(2,1)S(1)} %get-tuple-element.25.refs_2_), channel_id=1, source_target_pairs={{0,3},{1,0},{2,1},{3,2},{4,7},{5,4},{6,5},{7,6},{8,11},{9,8},{10,9... | collective-permute-start | bytes 1179656 | tf_op jit(solution)/shard_map/ppermute | solution.py:495
  85.2 0.1 pad_add_fusion.refs_0_.meta_ref
  85.3 9.0 %inner_windows.1.inner_hbm = f32[24,16,1024]{2,1,0:T(8,128)S(1)} custom-call(s32[3]{0:T(128)S(1)} %pad_add_fusion.refs_0_.meta_ref, bf16[768,1024]{1,0:T(8,128)(2,1)} %get-tuple-element.26.refs_1_, bf16[1024,3072]{1,0:T(8,128)(2,1)} %qkv_hbm.1), custom_call_target="tpu_custom_call" | custom-call | flops 3623878656 | bytes 12000000 | tf_op jit(solution)/shard_map/inner_windows/pallas_call | solution.py:351
  94.4 0.5 collective-permute-done.refs_1_
  94.9 0.0 collective-permute-done.1.refs_4_
  94.9 0.5 collective-permute-start.5
  95.4 0.0 copy-start.1
  95.4 0.0 copy-start.3
  95.4 1.4 collective-permute-start.4
  96.9 6.0 %edge_windows.1.edges_hbm = f32[16,16,1024]{2,1,0:T(8,128)S(1)} custom-call(s32[3]{0:T(128)S(1)} %pad_add_fusion.refs_0_.meta_ref, bf16[192,1024]{1,0:T(8,128)(2,1)S(1)} %collective-permute-done.refs_1_, bf16[192,1024]{1,0:T(8,128)(2,1)S(1)} %get-tuple-element.25.refs_2_, bf16[192,1024]{1,0:T(8,128)(2,1)S(1)} %get-tuple-element.24.refs_3_, ...), custom_call_target="tpu_custom_call" | custom-call | flops 2415919104 | bytes 12000000 | tf_op jit(solution)/shard_map/edge_windows/pallas_call | solution.py:351
  102.8 0.0 collective-permute-done.5.east_corners_ref
  102.9 19.9 %sides_decode.1 = bf16[128,128,128]{2,1,0:T(8,128)(2,1)S(1)} custom-call(s32[3]{0:T(128)S(1)} %pad_add_fusion.refs_0_.meta_ref, s32[128]{0:T(128)S(1)} %bitcast.22, s32[128,128]{1,0:T(8,128)S(1)} %get-tuple-element.20.cells_ref, bf16[768,1024]{1,0:T(8,128)(2,1)} %get-tuple-element.21.tokens_hbm, bf16[256,1024]{1,0:T(8,128)(2,1)S(1)} %get-tuple-element.22.west_ref, ...), custom_call_target="tpu_custom_call" | custom-call | flops 12000000000 | bytes 28000000 | tf_op jit(solution)/shard_map/sides_decode/pallas_call | solution.py:465
  122.8 61.6 %all_to_all.11 = bf16[128,1,128,128]{3,2,1,0:T(8,128)(2,1)S(1)} all-to-all(bf16[128,1,128,128]{3,2,1,0:T(8,128)(2,1)S(1)} %bitcast.16), channel_id=1, replica_groups=mesh['lon'=32,'lat'=4] {'lon','lat'}, dimensions={0} | all-to-all | bytes 8388608 | tf_op jit(solution)/shard_map/all_to_all | solution.py:551
  184.4 2.0 %copy.19 = bf16[128,1,128,128]{3,2,1,0:T(8,128)(2,1)} copy(bf16[128,1,128,128]{3,2,1,0:T(8,128)(2,1)S(1)} %all_to_all.11) | data formatting | bytes 8388608
  (12 shorter events, 0.1 us)
Async XLA Ops:
  6.7 64.6 %copy-start = (s32[128,1,128]{2,1,0:T(1,128)S(1)}, s32[128,1,128]{2,1,0:T(1,128)}, u32[]{:S(2)}) copy-start(s32[128,1,128]{2,1,0:T(1,128)} %param.17) | copy-start | bytes 196612
  6.7 64.5 %copy-start.2 = (f32[1024]{0:T(1024)S(1)}, f32[1024]{0:T(1024)}, u32[]{:S(2)}) copy-start(f32[1024]{0:T(1024)} %param.22) | copy-start | bytes 12292
  6.8 64.5 %copy-start.4 = (s32[128,1]{0,1:T(1,128)S(1)}, s32[128,1]{0,1:T(1,128)}, u32[]{:S(2)}) copy-start(s32[128,1]{0,1:T(1,128)} %param.18) | copy-start | bytes 1540
  71.3 13.9 %copy-start.5 = (s32[2]{0:T(128)S(1)}, s32[2]{0:T(128)}, u32[]{:S(2)}) copy-start(s32[2]{0:T(128)} %param.19) | copy-start | bytes 28
  80.7 14.1 %collective-permute-start.3 = (bf16[256,1024]{1,0:T(8,128)(2,1)S(1)}, bf16[256,1024]{1,0:T(8,128)(2,1)S(1)}, u32[]{:S(2)}, u32[]{:S(2)}) collective-permute-start(bf16[256,1024]{1,0:T(8,128)(2,1)S(1)} %get-tuple-element.22.west_ref), channel_id=1, source_target_pairs={{0,124},{1,125},{2,126},{3,127},{4,0},{5,1},{6,2},{7,3},{8,4},{9,5... | collective-permute-start | bytes 1572872 | tf_op jit(solution)/shard_map/ppermute | solution.py:495
  80.8 14.0 %collective-permute-start.2 = (bf16[256,1024]{1,0:T(8,128)(2,1)S(1)}, bf16[256,1024]{1,0:T(8,128)(2,1)S(1)}, u32[]{:S(2)}, u32[]{:S(2)}) collective-permute-start(bf16[256,1024]{1,0:T(8,128)(2,1)S(1)} %get-tuple-element.23.east_ref), channel_id=1, source_target_pairs={{0,4},{1,5},{2,6},{3,7},{4,8},{5,9},{6,10},{7,11},{8,12},{9,13},{1... | collective-permute-start | bytes 1572872 | tf_op jit(solution)/shard_map/ppermute | solution.py:495
  82.6 12.3 %collective-permute-start = (bf16[192,1024]{1,0:T(8,128)(2,1)S(1)}, bf16[192,1024]{1,0:T(8,128)(2,1)S(1)}, u32[]{:S(2)}, u32[]{:S(2)}) collective-permute-start(bf16[192,1024]{1,0:T(8,128)(2,1)S(1)} %get-tuple-element.24.refs_3_), channel_id=1, source_target_pairs={{0,1},{1,2},{2,3},{3,0},{4,5},{5,6},{6,7},{7,4},{8,9},{9,10},{10,1... | collective-permute-start | bytes 1179656 | tf_op jit(solution)/shard_map/ppermute | solution.py:495
  82.9 11.9 %collective-permute-start.1 = (bf16[192,1024]{1,0:T(8,128)(2,1)S(1)}, bf16[192,1024]{1,0:T(8,128)(2,1)S(1)}, u32[]{:S(2)}, u32[]{:S(2)}) collective-permute-start(bf16[192,1024]{1,0:T(8,128)(2,1)S(1)} %get-tuple-element.25.refs_2_), channel_id=1, source_target_pairs={{0,3},{1,0},{2,1},{3,2},{4,7},{5,4},{6,5},{7,6},{8,11},{9,8},{10,9... | collective-permute-start | bytes 1179656 | tf_op jit(solution)/shard_map/ppermute | solution.py:495
  94.9 7.9 %collective-permute-start.5 = (bf16[128,1024]{1,0:T(8,128)(2,1)S(1)}, bf16[128,1024]{1,0:T(8,128)(2,1)S(1)}, u32[]{:S(2)}, u32[]{:S(2)}) collective-permute-start(bf16[128,1024]{1,0:T(8,128)(2,1)S(1)} %pad_maximum_fusion.own_west_ref), channel_id=1, source_target_pairs={{0,124},{1,125},{2,126},{3,127},{4,0},{5,1},{6,2},{7,3},{8,4},{9,5... | collective-permute-start | bytes 786440 | tf_op jit(solution)/shard_map/ppermute | solution.py:495
  95.4 7.4 %copy-start.1 = (bf16[128,128]{1,0:T(8,128)(2,1)S(1)}, bf16[128,128]{1,0:T(8,128)(2,1)}, u32[]{:S(2)}) copy-start(bf16[128,128]{1,0:T(8,128)(2,1)} %read_ref.1) | copy-start | bytes 98308
  95.4 7.4 %copy-start.3 = (f32[1024]{0:T(1024)S(1)}, f32[1024]{0:T(1024)}, u32[]{:S(2)}) copy-start(f32[1024]{0:T(1024)} %param.25) | copy-start | bytes 12292
  95.4 7.4 %collective-permute-start.4 = (bf16[128,1024]{1,0:T(8,128)(2,1)S(1)}, bf16[128,1024]{1,0:T(8,128)(2,1)S(1)}, u32[]{:S(2)}, u32[]{:S(2)}) collective-permute-start(bf16[128,1024]{1,0:T(8,128)(2,1)S(1)} %pad_maximum_fusion.1.own_east_ref), channel_id=1, source_target_pairs={{0,4},{1,5},{2,6},{3,7},{4,8},{5,9},{6,10},{7,11},{8,12},{9,13},{1... | collective-permute-start | bytes 786440 | tf_op jit(solution)/shard_map/ppermute | solution.py:495
